TPU v7x, 128 devices: a whole 4x4x4 slice. The times are simulated.
128 devices in a mesh: hi: 8 (over x_hi, z), lo: 16 (over y, x_lo, core).
Axes of the slice: x: 4 (x_hi: 2, x_lo: 2; x = x_hi * 2 + x_lo), y: 4, z: 4, core: 2. Of those that a mesh axis runs over, the one named last changes fastest.
Arguments:
- amplitudes: float32 [8, 16, 131072], P('hi', 'lo'), may hold values from -6 to 6
- gate_stack: float32 [8, 128, 128], replicated, may hold values from -6 to 6
- targets: int32 [8, 7], replicated, may hold values from 0 to 9, as said below
Outputs:
- evolved: float32 [8, 16, 131072], P('hi', 'lo')
Inputs may be any that keep to these rules, and one draw needn't show every extreme that they name: `targets`: the seven entries of each row are distinct; the first row holds 0 and 9.
All inputs are finite; a program needn't handle non-finite values.
Results may differ from a plain program's by a relative error of at most 0.00019.
Values sent between devices are 32-bit elements; how exact they have to be, the bound alone decides.
No kernel may reach another device: no remote copies, remote signals or barrier semaphores. Data moves between devices by JAX's collectives and lax.ppermute only.
A program may use at most 64 MiB of HBM per device.

v0:
```python
import jax
import jax.numpy as jnp
from jax import lax
from jax.sharding import PartitionSpec as P

LAYERS = 8


def swapped(value, axis, stride):
    return lax.ppermute(value, axis, [(i, i ^ 1 << stride) for i in range(lax.axis_size(axis))])


def build_gates(gate_stack):
    layer_count = gate_stack.shape[0]
    order = gate_stack.shape[1]
    start = jnp.broadcast_to(jnp.eye(order, dtype=jnp.float32), (layer_count, order, order))

    def reflect(current, vectors):
        lengths = jnp.sum(vectors * vectors, axis=1)
        images = jnp.einsum("lij,lj->li", current, vectors, precision=lax.Precision.HIGHEST)
        scaled = images * (2.0 / lengths)[:, None]
        return (current - scaled[:, :, None] * vectors[:, None, :], None)

    result, unused = lax.scan(reflect, start, jnp.transpose(gate_stack, (1, 0, 2)))
    return result


def bit_moves(chosen, index_bits, picked):
    position_ids = jnp.arange(2**index_bits, dtype=jnp.int32)
    slot_ids = jnp.arange(picked, dtype=jnp.int32)
    source_index = jnp.zeros_like(position_ids)
    place_index = jnp.zeros_like(position_ids)
    for position in range(index_bits):
        matches = chosen == position
        slot_of = jnp.sum(jnp.where(matches, slot_ids, 0))
        lower_count = jnp.sum((chosen < position).astype(jnp.int32))
        new_place = jnp.where(jnp.any(matches), slot_of, picked + position - lower_count)
        source_index = source_index | (position_ids >> new_place & 1) << position
        place_index = place_index | (position_ids >> position & 1) << new_place
    return (source_index, place_index)


def apply_rows(blocks, gate_matrix):
    return jnp.dot(
        blocks, gate_matrix.T, precision=lax.Precision.HIGHEST, preferred_element_type=jnp.float32
    )


def local_layer(current, gate_matrix, chosen, row_bits):
    source_index, place_index = bit_moves(chosen, row_bits, 7)
    permuted = jnp.take(current, source_index, axis=1).reshape(-1, 128)
    permuted = apply_rows(permuted, gate_matrix).reshape(current.shape)
    return jnp.take(permuted, place_index, axis=1)


def lo_layer(current, gate_matrix, chosen, row_bits, lo_count):
    group_width = 128 // lo_count
    picked = 7 - (lo_count.bit_length() - 1)
    source_index, place_index = bit_moves(chosen[:picked], row_bits, picked)
    permuted = jnp.take(current, source_index, axis=1)
    blocks = permuted.reshape(lo_count, -1, group_width).transpose(1, 0, 2).reshape(-1, 128)
    blocks = apply_rows(blocks, gate_matrix)
    blocks = blocks.reshape(-1, lo_count, group_width).transpose(1, 0, 2).reshape(current.shape)
    return jnp.take(blocks, place_index, axis=1)


def bring_over(current):
    return lax.all_to_all(current, "lo", split_axis=0, concat_axis=0, tiled=True)


def send_home(current):
    return lax.all_to_all(current, "lo", split_axis=0, concat_axis=0, tiled=True)


def hi_layer(current, gate_matrix, chosen, row_bits, hi_bit):
    lo_count = current.shape[0]
    half_bit = lax.axis_index("hi") >> hi_bit & 1
    split_rows = current.reshape(lo_count, 2, -1)
    kept_half = lax.dynamic_index_in_dim(split_rows, half_bit, 1, keepdims=False)
    sent_half = lax.dynamic_index_in_dim(split_rows, 1 - half_bit, 1, keepdims=False)
    received = swapped(sent_half, "hi", hi_bit)
    source_index, place_index = bit_moves(chosen[:6], row_bits - 1, 6)
    low_part = jnp.take(
        jnp.where(half_bit == 0, kept_half, received), source_index, axis=1
    ).reshape(-1, 64)
    high_part = jnp.take(
        jnp.where(half_bit == 0, received, kept_half), source_index, axis=1
    ).reshape(-1, 64)
    mixed = apply_rows(jnp.concatenate([low_part, high_part], axis=1), gate_matrix)
    out_low = jnp.take(mixed[:, :64].reshape(lo_count, -1), place_index, axis=1)
    out_high = jnp.take(mixed[:, 64:].reshape(lo_count, -1), place_index, axis=1)
    own_new = jnp.where(half_bit == 0, out_low, out_high)
    returned = jnp.where(half_bit == 0, out_high, out_low)
    arrived = swapped(returned, "hi", hi_bit)
    stacked = jnp.where(
        half_bit == 0, jnp.stack([own_new, arrived], axis=1), jnp.stack([arrived, own_new], axis=1)
    )
    return stacked.reshape(lo_count, -1)


def body(amplitudes, gate_stack, targets):
    lo_count = lax.axis_size("lo")
    hi_bits = lax.axis_size("hi").bit_length() - 1
    amp_count = amplitudes.shape[2]
    row_count = amp_count // lo_count
    row_bits = row_count.bit_length() - 1
    gate_matrices = build_gates(gate_stack)
    current = amplitudes.reshape(lo_count, row_count)
    flipped = False
    for layer_index in range(LAYERS):
        gate_matrix = gate_matrices[layer_index]
        chosen = targets[layer_index]
        layer_kind = layer_index % 4
        if layer_kind == 0 or layer_kind == 2:
            current = local_layer(current, gate_matrix, chosen, row_bits)
        elif layer_kind == 1:
            hi_bit = layer_index // 4 % hi_bits
            current = hi_layer(current, gate_matrix, chosen, row_bits, hi_bit)
        else:
            current = send_home(
                lo_layer(bring_over(current), gate_matrix, chosen, row_bits, lo_count)
            )
    return current.reshape(1, 1, amp_count)


def solution(mesh):
    in_specs = (P("hi", "lo", None), P(), P())
    out_specs = P("hi", "lo", None)
    return jax.shard_map(body, mesh=mesh, in_specs=in_specs, out_specs=out_specs, check_vma=False)
```

profile of v0, /device:TPU:1, one launch (start us, length us, event | category | flops | bytes accessed | tf_op | source)
XLA Modules:
  0.0 1135.4 jit_solution(11577719798447724265)
XLA Ops:
  38.5 30.1 %gather_fusion = f32[8192,16]{1,0:T(8,128)} fusion(f32[16,8192]{0,1:T(8,128)} %copy.42, s32[8192]{0:T(1024)S(1)} %get-tuple-element.569), kind=kCustom, calls=%fused_computation.clone | custom fusion | bytes 1081344 | tf_op jit(solution)/shard_map/jit(_take)/gather | solution.py:51
  68.5 7.5 select_bitcast_fusion.9
  79.3 184.3 %while.10 = (s32[]{:T(128)}, f32[8,128,128]{2,1,0:T(8,128)S(1)}, f32[128,8,128]{2,1,0:T(8,128)S(1)}, s32[]{:T(128)}) while((s32[]{:T(128)}, f32[8,128,128]{2,1,0:T(8,128)S(1)}, f32[128,8,128]{2,1,0:T(8,128)S(1)}, s32[]{:T(128)}) %tuple.540), condition=%wide.region_41.43_spmd, body=%wide.region_39.42_spmd.sunk | while | flops 1838082 | bytes 1605817 | solution.py:24
  267.0 30.1 %gather_fusion.1 = f32[8192,16]{1,0:T(8,128)} fusion(f32[16,8192]{0,1:T(8,128)} %copy.45, s32[8192]{0:T(1024)S(1)} %get-tuple-element.568), kind=kCustom, calls=%fused_computation.2.clone | custom fusion | bytes 1081344 | tf_op jit(solution)/shard_map/jit(_take)/gather | solution.py:53
  343.6 15.8 %gather_fusion.3 = f32[4096,16]{1,0:T(8,128)} fusion(f32[16,4096]{0,1:T(8,128)} %get-tuple-element.341, s32[4096]{0:T(1024)S(1)} %get-tuple-element.573), kind=kCustom, calls=%fused_computation.13.clone | custom fusion | bytes 540672 | tf_op jit(solution)/shard_map/jit(_take)/gather | solution.py:86
  359.4 14.2 %gather_fusion.2 = f32[4096,16]{1,0:T(8,128)} fusion(f32[16,4096]{0,1:T(8,128)S(1)} %get-tuple-element.340, s32[4096]{0:T(1024)S(1)} %get-tuple-element.573), kind=kCustom, calls=%fused_computation.1.clone | custom fusion | bytes 540672 | tf_op jit(solution)/shard_map/jit(_take)/gather | solution.py:83
  384.5 14.2 %gather_fusion.4 = f32[4096,16]{1,0:T(8,128)} fusion(f32[16,4096]{0,1:T(8,128)S(1)} %copy.52, s32[4096]{0:T(1024)S(1)} %get-tuple-element.572), kind=kCustom, calls=%fused_computation.14.clone | custom fusion | bytes 540672 | tf_op jit(solution)/shard_map/jit(_take)/gather | solution.py:90
  398.7 15.8 %gather_fusion.5 = f32[4096,16]{1,0:T(8,128)} fusion(f32[16,4096]{0,1:T(8,128)} %copy.54, s32[4096]{0:T(1024)S(1)} %get-tuple-element.572), kind=kCustom, calls=%fused_computation.15.clone | custom fusion | bytes 540672 | tf_op jit(solution)/shard_map/jit(_take)/gather | solution.py:91
  474.0 29.9 %gather_fusion.6 = f32[8192,16]{1,0:T(8,128)} fusion(f32[16,8192]{0,1:T(8,128)} %bitcast.564, s32[8192]{0:T(1024)S(1)} %get-tuple-element.577), kind=kCustom, calls=%fused_computation.3.clone | custom fusion | bytes 1081344 | tf_op jit(solution)/shard_map/jit(_take)/gather | solution.py:51
  503.8 7.5 select_bitcast_fusion.8
  517.6 29.9 %gather_fusion.7 = f32[8192,16]{1,0:T(8,128)} fusion(f32[16,8192]{0,1:T(8,128)} %copy.60, s32[8192]{0:T(1024)S(1)} %get-tuple-element.576), kind=kCustom, calls=%fused_computation.4.clone | custom fusion | bytes 1081344 | tf_op jit(solution)/shard_map/jit(_take)/gather | solution.py:53
  547.5 7.5 select_bitcast_fusion.7
  566.0 9.5 all-to-all-done
  578.7 29.9 %gather_fusion.8 = f32[8192,16]{1,0:T(8,128)} fusion(f32[16,8192]{0,1:T(8,128)} %bitcast.565, s32[8192]{0:T(1024)S(1)} %broadcast_clamp_fusion.7), kind=kCustom, calls=%fused_computation.5.clone | custom fusion | bytes 1081344 | tf_op jit(solution)/shard_map/jit(_take)/gather | solution.py:60
  608.6 7.5 select_bitcast_fusion.6
  622.4 29.9 %gather_fusion.9 = f32[8192,16]{1,0:T(8,128)} fusion(f32[16,8192]{0,1:T(8,128)} %bitcast.566, s32[8192]{0:T(1024)S(1)} %broadcast_clamp_fusion.6), kind=kCustom, calls=%fused_computation.6.clone | custom fusion | bytes 1081344 | tf_op jit(solution)/shard_map/jit(_take)/gather | solution.py:64
  652.2 7.5 select_bitcast_fusion.5
  696.6 29.9 %gather_fusion.10 = f32[8192,16]{1,0:T(8,128)} fusion(f32[16,8192]{0,1:T(8,128)} %bitcast.567, s32[8192]{0:T(1024)S(1)} %broadcast_clamp_fusion.5), kind=kCustom, calls=%fused_computation.7.clone | custom fusion | bytes 1081344 | tf_op jit(solution)/shard_map/jit(_take)/gather | solution.py:51
  726.5 7.5 select_bitcast_fusion.4
  740.2 29.9 %gather_fusion.11 = f32[8192,16]{1,0:T(8,128)} fusion(f32[16,8192]{0,1:T(8,128)} %copy.70, s32[8192]{0:T(1024)S(1)} %broadcast_clamp_fusion.4), kind=kCustom, calls=%fused_computation.8.clone | custom fusion | bytes 1081344 | tf_op jit(solution)/shard_map/jit(_take)/gather | solution.py:53
  811.2 15.7 %gather_fusion.13 = f32[4096,16]{1,0:T(8,128)} fusion(f32[16,4096]{0,1:T(8,128)} %get-tuple-element.339, s32[4096]{0:T(1024)S(1)} %get-tuple-element.585), kind=kCustom, calls=%fused_computation.17.clone | custom fusion | bytes 540672 | tf_op jit(solution)/shard_map/jit(_take)/gather | solution.py:86
  826.9 14.1 %gather_fusion.12 = f32[4096,16]{1,0:T(8,128)} fusion(f32[16,4096]{0,1:T(8,128)S(1)} %get-tuple-element.338, s32[4096]{0:T(1024)S(1)} %get-tuple-element.585), kind=kCustom, calls=%fused_computation.16.clone | custom fusion | bytes 540672 | tf_op jit(solution)/shard_map/jit(_take)/gather | solution.py:83
  851.9 14.1 %gather_fusion.14 = f32[4096,16]{1,0:T(8,128)} fusion(f32[16,4096]{0,1:T(8,128)S(1)} %copy.77, s32[4096]{0:T(1024)S(1)} %get-tuple-element.584), kind=kCustom, calls=%fused_computation.18.clone | custom fusion | bytes 540672 | tf_op jit(solution)/shard_map/jit(_take)/gather | solution.py:90
  865.9 15.7 %gather_fusion.15 = f32[4096,16]{1,0:T(8,128)} fusion(f32[16,4096]{0,1:T(8,128)} %copy.79, s32[4096]{0:T(1024)S(1)} %get-tuple-element.584), kind=kCustom, calls=%fused_computation.19.clone | custom fusion | bytes 540672 | tf_op jit(solution)/shard_map/jit(_take)/gather | solution.py:91
  915.6 29.9 %gather_fusion.16 = f32[8192,16]{1,0:T(8,128)} fusion(f32[16,8192]{0,1:T(8,128)} %bitcast.568, s32[8192]{0:T(1024)S(1)} %get-tuple-element.589), kind=kCustom, calls=%fused_computation.9.clone | custom fusion | bytes 1081344 | tf_op jit(solution)/shard_map/jit(_take)/gather | solution.py:51
  945.5 7.5 select_bitcast_fusion.3
  959.3 29.9 %gather_fusion.17 = f32[8192,16]{1,0:T(8,128)} fusion(f32[16,8192]{0,1:T(8,128)} %copy.85, s32[8192]{0:T(1024)S(1)} %get-tuple-element.588), kind=kCustom, calls=%fused_computation.10.clone | custom fusion | bytes 1081344 | tf_op jit(solution)/shard_map/jit(_take)/gather | solution.py:53
  989.1 7.5 select_bitcast_fusion.2
  1034.6 29.9 %gather_fusion.18 = f32[8192,16]{1,0:T(8,128)} fusion(f32[16,8192]{0,1:T(8,128)} %bitcast.569, s32[8192]{0:T(1024)S(1)} %broadcast_clamp_fusion.1), kind=kCustom, calls=%fused_computation.11.clone | custom fusion | bytes 1081344 | tf_op jit(solution)/shard_map/jit(_take)/gather | solution.py:60
  1078.2 29.9 %gather_fusion.19 = f32[8192,16]{1,0:T(8,128)} fusion(f32[16,8192]{0,1:T(8,128)} %bitcast.570, s32[8192]{0:T(1024)S(1)} %broadcast_clamp_fusion), kind=kCustom, calls=%fused_computation.12.clone | custom fusion | bytes 1081344 | tf_op jit(solution)/shard_map/jit(_take)/gather | solution.py:64
  1108.1 7.5 select_bitcast_fusion
  1119.1 15.3 %all_to_all.45 = f32[16,1,8192]{2,1,0:T(1,128)S(1)} all-to-all(f32[16,1,8192]{2,1,0:T(1,128)S(1)} %copy.92), channel_id=1, replica_groups=mesh['hi'=8,'lo'=16] {'lo'}, dimensions={0} | all-to-all | bytes 1048576 | tf_op jit(solution)/shard_map/all_to_all | solution.py:72
  (776 shorter events, 370.7 us)
Async XLA Ops:
  76.0 2.9 copy-start.1
  304.5 5.0 copy-start.2
  306.8 30.9 %collective-permute-start = (f32[16,4096]{1,0:T(8,128)S(1)}, f32[16,4096]{1,0:T(8,128)S(1)}, u32[]{:S(2)}, u32[]{:S(2)}) collective-permute-start(f32[16,4096]{1,0:T(8,128)S(1)} %bitcast.576), channel_id=1, source_target_pairs={{0,16},{16,0},{32,48},{48,32},{64,80},{80,64},{96,112},{112,96},{1... | collective-permute-start | bytes 786440 | tf_op jit(solution)/shard_map/ppermute | solution.py:10
  420.1 51.0 %collective-permute-start.1 = (f32[16,4096]{1,0:T(8,128)S(1)}, f32[16,4096]{1,0:T(8,128)S(1)}, u32[]{:S(2)}, u32[]{:S(2)}) collective-permute-start(f32[16,4096]{1,0:T(8,128)S(1)} %copy.55), channel_id=1, source_target_pairs={{0,16},{16,0},{32,48},{48,32},{64,80},{80,64},{96,112},{112,96},{1... | collective-permute-start | bytes 786440 | tf_op jit(solution)/shard_map/ppermute | solution.py:10
  559.2 16.2 %all-to-all-start = ((f32[16,1,8192]{2,1,0:T(1,128)}), f32[16,1,8192]{2,1,0:T(1,128)S(1)}, u32[]{:S(2)}, u32[]{:S(2)}) async-start(f32[16,1,8192]{2,1,0:T(1,128)} %copy.61), calls=%async_computation | async-start | bytes 1048576 | tf_op jit(solution)/shard_map/all_to_all | solution.py:68
  664.0 29.4 %all-to-all-start.1 = ((f32[16,1,8192]{2,1,0:T(1,128)}), f32[16,1,8192]{2,1,0:T(1,128)S(1)}, u32[]{:S(2)}, u32[]{:S(2)}) async-start(f32[16,1,8192]{2,1,0:T(1,128)} %copy.67), calls=%async_computation.1 | async-start | bytes 1048576 | tf_op jit(solution)/shard_map/all_to_all | solution.py:72
  776.4 2.0 copy-start
  779.1 26.3 %collective-permute-start.2 = (f32[16,4096]{1,0:T(8,128)S(1)}, f32[16,4096]{1,0:T(8,128)S(1)}, u32[]{:S(2)}, u32[]{:S(2)}) collective-permute-start(f32[16,4096]{1,0:T(8,128)S(1)} %bitcast.577), channel_id=1, source_target_pairs={{0,32},{16,48},{32,0},{48,16},{64,96},{80,112},{96,64},{112,80},{1... | collective-permute-start | bytes 786440 | tf_op jit(solution)/shard_map/ppermute | solution.py:10
  887.3 25.5 %collective-permute-start.3 = (f32[16,4096]{1,0:T(8,128)S(1)}, f32[16,4096]{1,0:T(8,128)S(1)}, u32[]{:S(2)}, u32[]{:S(2)}) collective-permute-start(f32[16,4096]{1,0:T(8,128)S(1)} %copy.80), channel_id=1, source_target_pairs={{0,32},{16,48},{32,0},{48,16},{64,96},{80,112},{96,64},{112,80},{1... | collective-permute-start | bytes 786440 | tf_op jit(solution)/shard_map/ppermute | solution.py:10
  1000.9 30.6 %all-to-all-start.2 = ((f32[16,1,8192]{2,1,0:T(1,128)}), f32[16,1,8192]{2,1,0:T(1,128)S(1)}, u32[]{:S(2)}, u32[]{:S(2)}) async-start(f32[16,1,8192]{2,1,0:T(1,128)} %copy.86), calls=%async_computation.2 | async-start | bytes 1048576 | tf_op jit(solution)/shard_map/all_to_all | solution.py:68
where the time goes:
time: 1150 us; the launch traced here: 1140 us
  local copies, waits for them, and re-layouts  576 us (50%)
  other arithmetic  192 us (17%)
  between operations  191 us (17%)
  matrix products  123 us (11%)
  starting transfers between devices  24.4 us (2%)
  blocking collectives  15.3 us (1%)
    gather x4, local copies, waits for them, and re-layouts, local_layer(): return jnp.take(permuted, place_index, axis=1)  120 us
    gather x4, local copies, waits for them, and re-layouts, local_layer(): permuted = jnp.take(current, source_index, axis=1).reshape(-1, 128)  120 us
    dot_general x128, matrix products, reflect(): jnp.einsum('lij,lj->li', current, vectors, precision=lax.Precision.HIGHEST)  118 us
    gather x2, local copies, waits for them, and re-layouts, lo_layer(): permuted = jnp.take(current, source_index, axis=1)  59.7 us
    gather x2, local copies, waits for them, and re-layouts, lo_layer(): return jnp.take(blocks, place_index, axis=1)  59.7 us
    sub x128, other arithmetic, reflect(): return (current - scaled[:, :, None] * vectors[:, None, :], None)  37.6 us
    gather x2, local copies, waits for them, and re-layouts, hi_layer(): jnp.take(mixed[:, 64:].reshape(lo_count, -1), place_index, axis=1)  31.4 us
    gather x2, local copies, waits for them, and re-layouts, hi_layer(): jnp.take(jnp.where(half_bit == 0, received, kept_half), source_index, axi...  31.4 us
  transfers between devices with their start and end apart: 7, of which 1 were waited for; matrix products, arithmetic and copies ran while one was open for 1% of the time, Pallas kernels for 0%

commit v1 on v0

v1 whole, which is shorter than its diff:
```python
import jax
import jax.numpy as jnp
from jax import lax
from jax.experimental import pallas as pl
from jax.experimental.pallas import tpu as pltpu
from jax.sharding import Mesh
from jax.sharding import PartitionSpec as P

LAYERS = 8
SPAN = 10
WIDE = 1 << SPAN
GATE = 128
F32 = jnp.float32
BF16 = jnp.bfloat16
ROWS = 128
PICKED = (7, 6, 7, 3)


def two_parts(value):
    high = value.astype(BF16)
    return high, (value - high.astype(F32)).astype(BF16)


def three_parts(value):
    high = value.astype(BF16)
    left = value - high.astype(F32)
    middle = left.astype(BF16)
    return high, middle, (left - middle.astype(F32)).astype(BF16)


def dot(left, right):
    return lax.dot_general(left, right, (((1,), (0,)), ((), ())), preferred_element_type=F32)


def left_form(value):
    high, middle, low = three_parts(value)
    return jnp.concatenate([high, middle], 1), jnp.concatenate([high, low], 1)


def right_form(value):
    high, middle, low = three_parts(value)
    both = jnp.concatenate([high, middle], 1)
    return jnp.concatenate([both, both], 0), jnp.concatenate([low, high], 0)


def full_dot(left, right):
    first = dot(left[0], right[0])
    return first[:, :GATE] + (first[:, GATE:] + dot(left[1], right[1]))


def bit_places(targets_ref, layer):
    kind = layer % 4
    picked = PICKED[kind]
    chosen = [targets_ref[layer, j] for j in range(picked)]
    rest = []
    count = SPAN - picked
    taken = [sum((chosen[j] == q).astype(jnp.int32) for j in range(picked)) for q in range(SPAN)]
    rank = []
    free = jnp.int32(0)
    for q in range(SPAN):
        rank.append(free)
        free = free + 1 - taken[q]
    for k in range(count):
        place = jnp.int32(0)
        for q in range(SPAN):
            place = place + jnp.where((rank[q] == k) & (taken[q] == 0), q, 0)
        rest.append(place)
    return rest + chosen if kind == 3 else chosen + rest


def natural(position, places, low, high):
    value = jnp.zeros_like(position)
    for m in range(low, high):
        value = value + (((position >> m) & 1) << places[m])
    return value


def prepare_kernel(targets_ref, stack_ref, moves_ref, gates_ref, moved, state, low_tri, sems):
    identity = list(range(SPAN))
    places = [identity] + [bit_places(targets_ref, layer) for layer in range(LAYERS)] + [identity]
    lanes = lax.broadcasted_iota(jnp.int32, (16, WIDE), 1)
    subs = lax.broadcasted_iota(jnp.int32, (16, WIDE), 0)
    copies = []
    for k in range(LAYERS + 1):
        slot = k % 2
        if k >= 2:
            copies[k - 2].wait()
        source, target = places[k], places[k + 1]
        wanted = natural(lanes, target, 0, SPAN) - natural(subs, source, 0, 4)

        def rows(block, carry, source=source, wanted=wanted, slot=slot):
            base = natural(block * 16, source, 4, SPAN)
            moved[slot, pl.ds(pl.multiple_of(block * 16, 16), 16), :] = jnp.where(wanted == base, 1.0, 0.0).astype(BF16)
            return carry

        lax.fori_loop(0, WIDE // 16, rows, 0)
        copy = pltpu.make_async_copy(moved.at[slot], moves_ref.at[k], sems.at[slot])
        copy.start()
        copies.append(copy)
    row = lax.broadcasted_iota(jnp.int32, (GATE, GATE), 0)
    col = lax.broadcasted_iota(jnp.int32, (GATE, GATE), 1)
    shuffle = (row == ((col & 15) << 3 | col >> 4)).astype(F32)
    shuffle_right = right_form(shuffle)
    units, units_t = [], []
    for g in range(LAYERS):
        vectors = stack_ref[g]
        lengths = jnp.sum(vectors * vectors, axis=1, keepdims=True)
        unit = vectors * lax.rsqrt(lengths)
        if g % 4 == 3:
            unit = full_dot(left_form(unit), shuffle_right)
        units.append(unit)
        units_t.append(unit.T)
    for g in range(LAYERS):
        gram = full_dot(left_form(units[g]), right_form(units_t[g]))
        low_tri[g] = gram
        state[g] = jnp.where(row == col, 2.0 / gram, 0.0)

    def level(step, carry):
        bit = jnp.int32(1) << step
        same = (row >> (step + 1)) == (col >> (step + 1))
        row_set = (row & bit) != 0
        col_set = (col & bit) != 0
        lower = same & row_set & ~col_set
        upper = same & col_set & ~row_set
        for g in range(LAYERS):
            cut = jnp.where(upper if g % 4 == 3 else lower, low_tri[g], 0.0)
            now = state[g]
            first = full_dot(left_form(now), right_form(cut))
            state[g] = now - full_dot(left_form(first), right_form(now))
        return carry

    lax.fori_loop(0, 7, level, 0)
    lane_low = col < 64
    for g in range(LAYERS):
        inner = full_dot(left_form(state[g]), right_form(units[g]))
        gate = jnp.where(row == col, 1.0, 0.0) - full_dot(left_form(units_t[g]), right_form(inner))
        high, low = two_parts(gate)
        if g % 4 == 3:
            gates_ref[g, 0, :GATE, :] = jnp.concatenate([high, high], 1)
            gates_ref[g, 0, GATE:, :] = jnp.concatenate([low, low], 1)
        elif g % 4 == 1:
            turned = pltpu.roll(gate, 64, 1)
            for b in range(2):
                own = gate[64 * b : 64 * b + 64]
                other = turned[64 * b : 64 * b + 64]
                left = lane_low[:64]
                for a in range(2):
                    twice = jnp.where(left, own, other) if a == 0 else jnp.where(left, other, own)
                    block = jnp.concatenate([jnp.where(left, twice, 0.0), jnp.where(left, 0.0, twice)], 0)
                    parts = two_parts(block)
                    for part in range(2):
                        gates_ref[g, part, GATE * b : GATE * (b + 1), GATE * a : GATE * (a + 1)] = parts[part]
        else:
            both = jnp.concatenate([high, low], 1)
            gates_ref[g, 0, :GATE, :] = both
            gates_ref[g, 0, GATE:, :] = both
    copies[-2].wait()
    copies[-1].wait()


def prepare(targets, gate_stack):
    return pl.pallas_call(
        prepare_kernel,
        out_shape=(
            jax.ShapeDtypeStruct((LAYERS + 1, WIDE, WIDE), BF16),
            jax.ShapeDtypeStruct((LAYERS, 2, 2 * GATE, 2 * GATE), BF16),
        ),
        in_specs=[pl.BlockSpec(memory_space=pltpu.SMEM), pl.BlockSpec(memory_space=pltpu.VMEM)],
        out_specs=(pl.BlockSpec(memory_space=pl.ANY), pl.BlockSpec(memory_space=pltpu.VMEM)),
        scratch_shapes=[
            pltpu.VMEM((2, WIDE, WIDE), BF16),
            pltpu.VMEM((LAYERS, GATE, GATE), F32),
            pltpu.VMEM((LAYERS, GATE, GATE), F32),
            pltpu.SemaphoreType.DMA((2,)),
        ],
        compiler_params=pltpu.CompilerParams(vmem_limit_bytes=24 * 2**20),
        cost_estimate=pl.CostEstimate(flops=8 * 10**9, bytes_accessed=20 * 2**20, transcendentals=0),
        name="prepare",
    )(targets, gate_stack)


def evolve_kernel(x_ref, gates_ref, moves_hbm, out_ref, moves, now, then, sems):
    def fetch(k):
        return pltpu.make_async_copy(moves_hbm.at[k], moves.at[k % 3], sems.at[k % 3])

    fetch(0).start()
    fetch(1).start()
    for s in range(2):
        for tile in range(8):
            high, low = two_parts(x_ref[:, s * 8 + tile, :])
            lanes = slice(tile * 128, tile * 128 + 128)
            now[64 * s : 64 * s + 64, lanes] = high
            now[ROWS + 64 * s : ROWS + 64 * s + 64, lanes] = low

    def lanes_of(n):
        return pl.ds(pl.multiple_of(n * 256, 256), 256)

    for k in range(LAYERS + 1):
        if k + 2 <= LAYERS:
            fetch(k + 2).start()
        fetch(k).wait()
        move = moves.at[k % 3]
        source, target = (now, then) if k % 2 == 0 else (then, now)
        kind = 4 if k == LAYERS else k % 4

        def block(n, carry, k=k, kind=kind, move=move, source=source, target=target):
            moved = dot(source[...], move[:, lanes_of(n)])
            if kind == 4:
                total = moved[:ROWS] + moved[ROWS:]
                for half in range(2):
                    for s in range(2):
                        out_ref[:, s * 8 + n * 2 + half, :] = total[64 * s : 64 * s + 64, 128 * half : 128 * half + 128]
                return carry
            moved = moved.astype(BF16)
            if kind == 3:
                target[:, lanes_of(n)] = moved
                return carry
            high, low = moved[:ROWS], moved[ROWS:]
            if kind == 1:
                width = 16 << (k // 4)
                groups = ROWS // (2 * width)
                zero = [slice(2 * width * i, 2 * width * i + width) for i in range(groups)]
                one = [slice(2 * width * i + width, 2 * width * (i + 1)) for i in range(groups)]

                def pairs(part):
                    sides = []
                    for rows in (zero, one):
                        sides.append(jnp.concatenate([part[r, 128 * half : 128 * half + 128] for half in range(2) for r in rows], 0))
                    return jnp.concatenate(sides, 1)

                high_pairs, low_pairs = pairs(high), pairs(low)
                out = dot(high_pairs, gates_ref[k, 0]) + dot(low_pairs, gates_ref[k, 0]) + dot(high_pairs, gates_ref[k, 1])
                halves = []
                for half in range(2):
                    pieces = []
                    for i in range(groups):
                        rows = slice(64 * half + width * i, 64 * half + width * (i + 1))
                        pieces += [out[rows, :128], out[rows, 128:]]
                    halves.append(jnp.concatenate(pieces, 0))
                result = jnp.concatenate(halves, 1)
            else:
                tall = jnp.concatenate(
                    [jnp.concatenate([high[:, 128 * h : 128 * h + 128], low[:, 128 * h : 128 * h + 128]], 1) for h in range(2)], 0
                )
                out = dot(tall, gates_ref[k, 0])
                out = out[:, :128] + out[:, 128:]
                result = jnp.concatenate([out[:ROWS], out[ROWS:]], 1)
            high, low = two_parts(result)
            target[:ROWS, lanes_of(n)] = high
            target[ROWS:, lanes_of(n)] = low
            return carry

        if kind == 4:
            for n in range(4):
                block(n, 0)
        else:
            lax.fori_loop(0, 4, block, 0)
        if kind == 3:
            for q in range(0, 8, 2):
                columns = []
                for p in (q, q + 1):
                    rows = [target[part * ROWS + 16 * p : part * ROWS + 16 * p + 16, 128 * t : 128 * t + 128] for part in range(2) for t in range(8)]
                    columns.append(jnp.concatenate(rows, 0))
                out = dot(gates_ref[k, 0], jnp.concatenate(columns, 1))
                high, low = two_parts(out[:ROWS] + out[ROWS:])
                for i, p in enumerate((q, q + 1)):
                    for t in range(8):
                        rows, lanes = slice(16 * t, 16 * t + 16), slice(128 * i, 128 * i + 128)
                        target[16 * p : 16 * p + 16, 128 * t : 128 * t + 128] = high[rows, lanes]
                        target[ROWS + 16 * p : ROWS + 16 * p + 16, 128 * t : 128 * t + 128] = low[rows, lanes]


def evolve(state, gates, moves):
    return pl.pallas_call(
        evolve_kernel,
        out_shape=jax.ShapeDtypeStruct(state.shape, F32),
        in_specs=[
            pl.BlockSpec(memory_space=pltpu.VMEM),
            pl.BlockSpec(memory_space=pltpu.VMEM),
            pl.BlockSpec(memory_space=pl.ANY),
        ],
        out_specs=pl.BlockSpec(memory_space=pltpu.VMEM),
        scratch_shapes=[
            pltpu.VMEM((3, WIDE, WIDE), BF16),
            pltpu.VMEM((2 * ROWS, WIDE), BF16),
            pltpu.VMEM((2 * ROWS, WIDE), BF16),
            pltpu.SemaphoreType.DMA((3,)),
        ],
        compiler_params=pltpu.CompilerParams(vmem_limit_bytes=24 * 2**20),
        cost_estimate=pl.CostEstimate(flops=6 * 10**9, bytes_accessed=20 * 2**20, transcendentals=0),
        name="evolve",
    )(state, gates, moves)


def body(amplitudes, gate_stack, targets):
    group = ("z", "lo")
    state = amplitudes.reshape(64, 16, 128)
    state = lax.all_to_all(state, group, split_axis=0, concat_axis=0, tiled=True)
    moves, gates = prepare(targets, gate_stack)
    state = evolve(state, gates, moves)
    state = lax.all_to_all(state, group, split_axis=0, concat_axis=0, tiled=True)
    return state.reshape(amplitudes.shape)


def solution(mesh):
    split = Mesh(mesh.devices.reshape(2, 4, 16), ("top", "z", "lo"))
    in_specs = (P(("top", "z"), "lo", None), P(), P())
    out_specs = P(("top", "z"), "lo", None)
    return jax.shard_map(body, mesh=split, in_specs=in_specs, out_specs=out_specs, check_vma=False)
```

time: 1150 us -> 94.3 us (0.08); the launches traced: 1140 us -> 93.9 us
  local copies, waits for them, and re-layouts: 576 us -> 15.3 us
  other arithmetic: 192 us -> 0 us
  between operations: 191 us -> 0.04 us
  matrix products: 123 us -> 0 us
  Pallas kernels: 0 us -> 46.2 us
  starting transfers between devices: 24.4 us -> 10.9 us
    gather x20 -> x0, local copies, waits for them, and re-layouts: 478 us -> none  [the longest x4 120 us: local_layer(): return jnp.take(permuted, place_index, axis=1)]
    dot_general x136 -> x0, matrix products: 123 us -> none  [the longest x128 118 us: reflect(): jnp.einsum('lij,lj->li', current, vectors, precision=lax.Precision.HIGHEST)]
    select_n x12 -> x0, other arithmetic: 58.4 us -> none  [the longest x4 29.9 us: local_layer(): permuted = jnp.take(current, source_index, axis=1).reshape(-1, 128)]
    pallas_call x0 -> x2, Pallas kernels: none -> 46.2 us  [the longest x1 26.7 us: prepare(): pl.pallas_call(prepare_kernel, out_shape=(jax.ShapeDtypeStruct((LAYERS +...]
    sub x128 -> x0, other arithmetic: 37.6 us -> none  [reflect(): return (current - scaled[:, :, None] * vectors[:, None, :], None)]
    all_to_all x4 -> x0, other arithmetic: 29.9 us -> none  [the longest x2 14.9 us: send_home(): lax.all_to_all(current, 'lo', split_axis=0, concat_axis=0, tiled=True)]
    reshape x28 -> x0, local copies, waits for them, and re-layouts: 27.3 us -> none  [the longest x8 11.3 us: local_layer(): permuted = apply_rows(permuted, gate_matrix).reshape(current.shape)]
    select_n x12 -> x0, local copies, waits for them, and re-layouts: 26.5 us -> none  [the longest x4 11.2 us: local_layer(): permuted = jnp.take(current, source_index, axis=1).reshape(-1, 128)]
  transfers between devices with their start and end apart: 7 -> 1, of which waited for: 1 -> 0; matrix products, arithmetic and copies ran while one was open for 1% -> 0% of each run, Pallas kernels for 0% -> 28%
where the time goes in v1:
time: 94.3 us; the launch traced here: 93.9 us
  Pallas kernels  46.2 us (49%)
  blocking collectives  21.4 us (23%)
  local copies, waits for them, and re-layouts  15.3 us (16%)
  starting transfers between devices  10.9 us (12%)
    pallas_call x1, Pallas kernels, prepare(): pl.pallas_call(prepare_kernel, out_shape=(jax.ShapeDtypeStruct((LAYERS +...  26.7 us
    all_to_all x1, blocking collectives, body(): lax.all_to_all(state, group, split_axis=0, concat_axis=0, tiled=True)  21.4 us
    pallas_call x1, Pallas kernels, evolve(): pl.pallas_call(evolve_kernel, out_shape=jax.ShapeDtypeStruct(state.shape,...  19.5 us
    unnamed x9, local copies, waits for them, and re-layouts  15.3 us
    all_to_all x1, starting transfers between devices, body(): lax.all_to_all(state, group, split_axis=0, concat_axis=0, tiled=True)  10.9 us
  transfers between devices with their start and end apart: 1, of which 0 were waited for; matrix products, arithmetic and copies ran while one was open for 0% of the time, Pallas kernels for 28%

profile of v1, /device:TPU:1, one launch (start us, length us, event | category | flops | bytes accessed | tf_op | source)
XLA Modules:
  0.0 93.9 jit_solution(12104649410462464936)
XLA Ops:
  0.0 10.9 %all-to-all-start = ((f32[64,16,128]{2,1,0:T(8,128)}), f32[64,16,128]{2,1,0:T(8,128)S(1)}, u32[]{:S(2)}, u32[]{:S(2)}) async-start(f32[64,16,128]{2,1,0:T(8,128)} %bitcast.3), calls=%async_computation | async-start | bytes 1048576 | tf_op jit(solution)/shard_map/all_to_all | solution.py:298
  10.9 0.0 copy-start
  11.0 1.0 %copy-done = f32[8,128,128]{2,1,0:T(8,128)S(1)} copy-done((f32[8,128,128]{2,1,0:T(8,128)S(1)}, f32[8,128,128]{2,1,0:T(8,128)}, u32[]{:S(2)}) %copy-start) | copy-done | bytes 524312
  12.0 0.0 copy-start.1
  12.0 0.7 copy-done.1
  12.7 26.7 %prepare.1 = (bf16[9,1024,1024]{2,1,0:T(8,128)(2,1)S(1)}, bf16[8,2,256,256]{3,2,1,0:T(8,128)(2,1)S(1)}) custom-call(s32[8,7]{1,0:T(8,128)S(1)} %copy-done.1, f32[8,128,128]{2,1,0:T(8,128)S(1)} %copy-done), custom_call_target="tpu_custom_call" | custom-call | flops 8000000000 | bytes 20971520 | tf_op jit(solution)/shard_map/prepare/pallas_call | solution.py:162
  39.4 0.0 copy-start.2
  39.4 6.5 %copy-done.2 = bf16[9,1024,1024]{2,1,0:T(8,128)(2,1)} copy-done((bf16[9,1024,1024]{2,1,0:T(8,128)(2,1)}, bf16[9,1024,1024]{2,1,0:T(8,128)(2,1)S(1)}, u32[]{:S(2)}) %copy-start.2) | copy-done | bytes 18874392
  45.9 0.0 all-to-all-done.x_ref
  45.9 0.0 copy-start.3
  45.9 6.4 %copy-done.3 = bf16[9,1024,1024]{2,1,0:T(8,128)(2,1)S(1)} copy-done((bf16[9,1024,1024]{2,1,0:T(8,128)(2,1)S(1)}, bf16[9,1024,1024]{2,1,0:T(8,128)(2,1)}, u32[]{:S(2)}) %copy-start.3) | copy-done | bytes 18874392
  52.2 19.5 %evolve.1 = f32[64,16,128]{2,1,0:T(8,128)S(1)} custom-call(f32[64,16,128]{2,1,0:T(8,128)S(1)} %all-to-all-done.x_ref, bf16[8,2,256,256]{3,2,1,0:T(8,128)(2,1)S(1)} %get-tuple-element.7.gates_ref, bf16[9,1024,1024]{2,1,0:T(8,128)(2,1)S(1)} %copy-done.3), custom_call_target="tpu_custom_call" | custom-call | flops 6000000000 | bytes 20971520 | tf_op jit(solution)/shard_map/evolve/pallas_call | solution.py:274
  71.7 21.4 %all_to_all.10 = f32[64,16,128]{2,1,0:T(8,128)S(1)} all-to-all(f32[64,16,128]{2,1,0:T(8,128)S(1)} %evolve.1), channel_id=1, replica_groups=mesh['top'=2,'z'=4,'lo'=16] {'z','lo'}, dimensions={0} | all-to-all | bytes 1048576 | tf_op jit(solution)/shard_map/all_to_all | solution.py:301
  93.1 0.8 copy.5
Async XLA Ops:
  0.0 45.9 %all-to-all-start = ((f32[64,16,128]{2,1,0:T(8,128)}), f32[64,16,128]{2,1,0:T(8,128)S(1)}, u32[]{:S(2)}, u32[]{:S(2)}) async-start(f32[64,16,128]{2,1,0:T(8,128)} %bitcast.3), calls=%async_computation | async-start | bytes 1048576 | tf_op jit(solution)/shard_map/all_to_all | solution.py:298
  10.9 1.0 %copy-start = (f32[8,128,128]{2,1,0:T(8,128)S(1)}, f32[8,128,128]{2,1,0:T(8,128)}, u32[]{:S(2)}) copy-start(f32[8,128,128]{2,1,0:T(8,128)} %stack_ref.1) | copy-start | bytes 1572868
  12.0 0.7 copy-start.1
  39.4 6.5 %copy-start.2 = (bf16[9,1024,1024]{2,1,0:T(8,128)(2,1)}, bf16[9,1024,1024]{2,1,0:T(8,128)(2,1)S(1)}, u32[]{:S(2)}) copy-start(bf16[9,1024,1024]{2,1,0:T(8,128)(2,1)S(1)} %get-tuple-element.8.moves_hbm) | copy-start | bytes 56623108
  45.9 6.4 %copy-start.3 = (bf16[9,1024,1024]{2,1,0:T(8,128)(2,1)S(1)}, bf16[9,1024,1024]{2,1,0:T(8,128)(2,1)}, u32[]{:S(2)}) copy-start(bf16[9,1024,1024]{2,1,0:T(8,128)(2,1)} %copy-done.2) | copy-start | bytes 56623108

commit v2 on v0

v2 whole, which is shorter than its diff:
```python
import jax
import jax.numpy as jnp
from jax import lax
from jax.experimental import pallas as pl
from jax.experimental.pallas import tpu as pltpu
from jax.sharding import Mesh
from jax.sharding import PartitionSpec as P

LAYERS = 8
SPAN = 10
WIDE = 1 << SPAN
GATE = 128
FULL = WIDE - 1
LANES = GATE - 1
F32 = jnp.float32
BF16 = jnp.bfloat16
I32 = jnp.int32
PICKED = (7, 6, 7, 3)


def two_parts(value):
    high = value.astype(BF16)
    return high, (value - high.astype(F32)).astype(BF16)


def three_parts(value):
    high = value.astype(BF16)
    left = value - high.astype(F32)
    middle = left.astype(BF16)
    return high, middle, (left - middle.astype(F32)).astype(BF16)


def dot(left, right):
    return lax.dot_general(left, right, (((1,), (0,)), ((), ())), preferred_element_type=F32)


def left_form(value):
    high, middle, low = three_parts(value)
    return jnp.concatenate([high, middle], 1), jnp.concatenate([high, low], 1)


def right_form(value):
    high, middle, low = three_parts(value)
    both = jnp.concatenate([high, middle], 1)
    return jnp.concatenate([both, both], 0), jnp.concatenate([low, high], 0)


def full_dot(left, right):
    first = dot(left[0], right[0])
    return first[:, :GATE] + (first[:, GATE:] + dot(left[1], right[1]))


def lowest(mask, count):
    bits = []
    for _ in range(count):
        low = mask & -mask
        bits.append(low)
        mask = mask ^ low
    return bits


def union(bits):
    mask = bits[0]
    for bit in bits[1:]:
        mask = mask | bit
    return mask


def layer_orders(targets_ref):
    masks, tops = [LANES], [[128, 256, 512]]
    targets = []
    for layer in range(LAYERS):
        kind = layer % 4
        picked = [jnp.int32(1) << targets_ref[layer, j] for j in range(PICKED[kind])]
        targets.append(picked)
        mask = union(picked)
        other = FULL ^ mask
        if kind == 3:
            masks.append(other)
            tops.append(picked)
        else:
            masks.append(mask)
            tops.append(lowest(other, SPAN - PICKED[kind]))
    masks.append(LANES)
    tops.append([128, 256, 512])
    shared = [lowest(masks[s] & masks[s + 1], 3) for s in range(LAYERS + 1)]

    def order(stage, low):
        return low + lowest(masks[stage] ^ union(low), SPAN - 3 - len(tops[stage])) + tops[stage]

    taken = [None] + [order(s, shared[s - 1]) for s in range(1, LAYERS + 2)]
    left = [order(s, shared[s]) for s in range(LAYERS + 1)] + [None]
    return targets, taken, left


def spread(position, bits):
    value = jnp.zeros_like(position)
    for m, bit in enumerate(bits):
        value = jnp.where((position & (1 << m)) != 0, value + bit, value)
    return value


def collect(value, bits):
    position = jnp.zeros_like(value)
    for m, bit in enumerate(bits):
        position = jnp.where((value & bit) != 0, position + (1 << m), position)
    return position


def prepare_kernel(targets_ref, stack_ref, gates_ref, moves_ref, perms_ref, state, gram_ref):
    lane = lax.broadcasted_iota(I32, (8, GATE), 1)
    targets, taken, left = layer_orders(targets_ref)
    for s in range(LAYERS + 1):
        source = collect(spread(lane, taken[s + 1][3:]), left[s][3:])
        moves_ref[s] = source * 8
    natural = [1 << m for m in range(7)]
    for i, (old, new) in enumerate(
        [(natural, left[0]), (taken[4], left[4]), (taken[8], left[8]), (taken[9], natural)]
    ):
        perms_ref[i] = collect(spread(lane, new[:7]), old[:7])
    row = lax.broadcasted_iota(I32, (GATE, GATE), 0)
    col = lax.broadcasted_iota(I32, (GATE, GATE), 1)
    ins, outs, deltas = [], [], []
    for g in range(LAYERS):
        vectors = stack_ref[g]
        lengths = jnp.sum(vectors * vectors, axis=1, keepdims=True)
        unit = vectors * lax.rsqrt(lengths)
        if g % 4 == 3:
            index_in = index_out = (lane & 15) << 3 | lane >> 4
        else:
            count = PICKED[g % 4]
            index_in, index_out = (
                collect(spread(lane, order[g + 1][:count]), targets[g]) + (lane >> count << count) for order in (taken, left)
            )
        pick_in = jnp.where(row == index_in[:1], 1.0, 0.0)
        pick_out = jnp.where(row == index_out[:1], 1.0, 0.0)
        out_rows = jnp.broadcast_to(index_out[:1], (GATE, GATE)).astype(F32).T
        deltas.append(jnp.where(out_rows == index_in[:1].astype(F32), 1.0, 0.0))
        parts = dot(jnp.concatenate(three_parts(unit), 0), jnp.concatenate([pick_in, pick_out], 1).astype(BF16))
        both = parts[:GATE] + parts[GATE : 2 * GATE] + parts[2 * GATE :]
        ins.append(both[:, :GATE])
        outs.append(both[:, GATE:].T)
        gram_ref[g] = full_dot(left_form(both[:, :GATE]), right_form(both[:, :GATE].T))
        state[g] = jnp.where(row == col, 2.0 / gram_ref[g], 0.0)

    def level(step, carry):
        bit = jnp.int32(1) << step
        upper = ((row >> (step + 1)) == (col >> (step + 1))) & ((col & bit) != 0) & ((row & bit) == 0)
        for g in range(LAYERS):
            cut = jnp.where(upper, gram_ref[g], 0.0)
            now = state[g]
            first = full_dot(left_form(now), right_form(cut))
            state[g] = now - full_dot(left_form(first), right_form(now))
        return carry

    lax.fori_loop(0, 7, level, 0)
    for g in range(LAYERS):
        inner = full_dot(left_form(state[g]), right_form(ins[g]))
        gate = deltas[g] - full_dot(left_form(outs[g]), right_form(inner))
        if g % 4 == 1:
            gate = jnp.where(row < 64, gate, pltpu.roll(gate, 64, 1))
        high, low = two_parts(gate)
        gates_ref[g, :GATE, :] = jnp.concatenate([high, high], 1)
        gates_ref[g, GATE:, :] = jnp.concatenate([low, low], 1)


def prepare(targets, gate_stack):
    return pl.pallas_call(
        prepare_kernel,
        out_shape=(
            jax.ShapeDtypeStruct((LAYERS, 2 * GATE, 2 * GATE), BF16),
            jax.ShapeDtypeStruct((LAYERS + 1, 8, GATE), I32),
            jax.ShapeDtypeStruct((4, 8, GATE), I32),
        ),
        in_specs=[pl.BlockSpec(memory_space=pltpu.SMEM), pl.BlockSpec(memory_space=pltpu.VMEM)],
        out_specs=(pl.BlockSpec(memory_space=pltpu.VMEM),) * 3,
        scratch_shapes=[
            pltpu.VMEM((LAYERS, GATE, GATE), F32),
            pltpu.VMEM((LAYERS, GATE, GATE), F32),
        ],
        compiler_params=pltpu.CompilerParams(vmem_limit_bytes=24 * 2**20),
        cost_estimate=pl.CostEstimate(flops=8 * 10**9, bytes_accessed=20 * 2**20, transcendentals=0),
        name="prepare",
    )(targets, gate_stack)


def side_by_side(blocks):
    return jnp.concatenate([jnp.concatenate(block, 0) for block in blocks], 1)


def evolve_kernel(x_ref, gates_ref, moves_ref, perms_ref, out_ref, here, there, table, sem):
    copy = pltpu.make_async_copy(moves_ref, table, sem)
    copy.start()
    lane = lax.broadcasted_iota(I32, (64, GATE), 1)

    def permuted(value, i):
        return jnp.take_along_axis(value, jnp.broadcast_to(perms_ref[i, :1, :], value.shape), axis=1)

    for tile in range(8):
        value = jnp.concatenate([x_ref[:, tile, :], x_ref[:, 8 + tile, :]], 0)
        here[tile * GATE : (tile + 1) * GATE, :] = permuted(value, 0).T
    copy.wait()

    def rows(source, stage, first, count):
        return jnp.concatenate(
            [source[pl.ds(pl.multiple_of(table[stage, 0, first + i], 8), 8), :] for i in range(count)], 0
        )

    def applied(layer, blocks):
        out = dot(gates_ref[layer], side_by_side(blocks))
        return out[:GATE] + out[GATE:]

    source, target = here, there
    for layer in range(LAYERS):
        kind = layer % 4
        if kind == 1:
            width = 16 << (layer // 4)
            one = (lane & width) != 0
            for pair in range(8):
                blocks = []
                for i in range(2):
                    own = rows(source, layer, (2 * pair + i) * 8, 8)
                    other = jnp.where(one, pltpu.roll(own, width, 1), pltpu.roll(own, GATE - width, 1))
                    own, other = two_parts(own), two_parts(other)
                    blocks.append([own[0], other[0], own[1], other[1]])
                out = applied(layer, blocks)
                for i in range(2):
                    first = (2 * pair + i) * 64
                    part = out[:, GATE * i : GATE * (i + 1)]
                    target[first : first + 64, :] = jnp.where(one, part[64:], part[:64])
        elif kind == 3:
            tiles = [two_parts(rows(source, layer, tile * 16, 16).T) for tile in range(8)]
            outs = []
            for q in range(0, 8, 2):
                blocks = [
                    [tiles[t][part][16 * p : 16 * p + 16] for part in range(2) for t in range(8)] for p in (q, q + 1)
                ]
                outs.append(applied(layer, blocks))
            for tile in range(8):
                value = jnp.concatenate(
                    [outs[q // 2][16 * tile : 16 * tile + 16, GATE * (q % 2) : GATE * (q % 2 + 1)] for q in range(8)], 0
                )
                target[tile * GATE : (tile + 1) * GATE, :] = permuted(value, 1 + layer // 4).T
        else:
            for pair in range(4):
                blocks = [two_parts(rows(source, layer, (2 * pair + i) * 16, 16)) for i in range(2)]
                out = applied(layer, blocks)
                for i in range(2):
                    first = (2 * pair + i) * GATE
                    target[first : first + GATE, :] = out[:, GATE * i : GATE * (i + 1)]
        source, target = target, source
    for tile in range(8):
        value = permuted(rows(source, LAYERS, tile * 16, 16).T, 3)
        out_ref[:, tile, :] = value[:64]
        out_ref[:, 8 + tile, :] = value[64:]


def evolve(state, gates, moves, perms):
    return pl.pallas_call(
        evolve_kernel,
        out_shape=jax.ShapeDtypeStruct(state.shape, F32),
        in_specs=[pl.BlockSpec(memory_space=pltpu.VMEM)] * 4,
        out_specs=pl.BlockSpec(memory_space=pltpu.VMEM),
        scratch_shapes=[
            pltpu.VMEM((WIDE, GATE), F32),
            pltpu.VMEM((WIDE, GATE), F32),
            pltpu.SMEM((LAYERS + 1, 8, GATE), I32),
            pltpu.SemaphoreType.DMA,
        ],
        compiler_params=pltpu.CompilerParams(vmem_limit_bytes=24 * 2**20),
        cost_estimate=pl.CostEstimate(flops=6 * 10**9, bytes_accessed=20 * 2**20, transcendentals=0),
        name="evolve",
    )(state, gates, moves, perms)


def body(amplitudes, gate_stack, targets):
    group = ("z", "lo")
    state = amplitudes.reshape(64, 16, 128)
    state = lax.all_to_all(state, group, split_axis=0, concat_axis=0, tiled=True)
    state = evolve(state, *prepare(targets, gate_stack))
    state = lax.all_to_all(state, group, split_axis=0, concat_axis=0, tiled=True)
    return state.reshape(amplitudes.shape)


def solution(mesh):
    split = Mesh(mesh.devices.reshape(2, 4, 16), ("top", "z", "lo"))
    in_specs = (P(("top", "z"), "lo", None), P(), P())
    out_specs = P(("top", "z"), "lo", None)
    return jax.shard_map(body, mesh=split, in_specs=in_specs, out_specs=out_specs, check_vma=False)
```

time: 1150 us -> 56.6 us (0.05); the launches traced: 1140 us -> 56.4 us
  local copies, waits for them, and re-layouts: 576 us -> 0.8 us
  other arithmetic: 192 us -> 0 us
  between operations: 191 us -> 0.05 us
  matrix products: 123 us -> 0 us
  Pallas kernels: 0 us -> 22.9 us
  starting transfers between devices: 24.4 us -> 11.1 us
    gather x20 -> x0, local copies, waits for them, and re-layouts: 478 us -> none  [the longest x4 120 us: local_layer(): return jnp.take(permuted, place_index, axis=1)]
    dot_general x136 -> x0, matrix products: 123 us -> none  [the longest x128 118 us: reflect(): jnp.einsum('lij,lj->li', current, vectors, precision=lax.Precision.HIGHEST)]
    select_n x12 -> x0, other arithmetic: 58.4 us -> none  [the longest x4 29.9 us: local_layer(): permuted = jnp.take(current, source_index, axis=1).reshape(-1, 128)]
    sub x128 -> x0, other arithmetic: 37.6 us -> none  [reflect(): return (current - scaled[:, :, None] * vectors[:, None, :], None)]
    all_to_all x4 -> x0, other arithmetic: 29.9 us -> none  [the longest x2 14.9 us: send_home(): lax.all_to_all(current, 'lo', split_axis=0, concat_axis=0, tiled=True)]
    reshape x28 -> x0, local copies, waits for them, and re-layouts: 27.3 us -> none  [the longest x8 11.3 us: local_layer(): permuted = apply_rows(permuted, gate_matrix).reshape(current.shape)]
    select_n x12 -> x0, local copies, waits for them, and re-layouts: 26.5 us -> none  [the longest x4 11.2 us: local_layer(): permuted = jnp.take(current, source_index, axis=1).reshape(-1, 128)]
    all_to_all x7 -> x0, local copies, waits for them, and re-layouts: 26 us -> none  [the longest x4 14.9 us: bring_over(): lax.all_to_all(current, 'lo', split_axis=0, concat_axis=0, tiled=True)]
  transfers between devices with their start and end apart: 7 -> 1, of which waited for: 1 -> 0; matrix products, arithmetic and copies ran while one was open for 1% -> 0% of each run, Pallas kernels for 0% -> 30%
where the time goes in v2:
time: 56.6 us; the launch traced here: 56.4 us
  Pallas kernels  22.9 us (40%)
  blocking collectives  21.5 us (38%)
  starting transfers between devices  11.1 us (20%)
  local copies, waits for them, and re-layouts  0.8 us (1%)
    all_to_all x1, blocking collectives, body(): lax.all_to_all(state, group, split_axis=0, concat_axis=0, tiled=True)  21.5 us
    pallas_call x1, Pallas kernels, prepare(): pl.pallas_call(prepare_kernel, out_shape=(jax.ShapeDtypeStruct((LAYERS, 2...  16.9 us
    all_to_all x1, starting transfers between devices, body(): lax.all_to_all(state, group, split_axis=0, concat_axis=0, tiled=True)  11.1 us
    pallas_call x1, Pallas kernels, evolve(): pl.pallas_call(evolve_kernel, out_shape=jax.ShapeDtypeStruct(state.shape,...  6.02 us
  transfers between devices with their start and end apart: 1, of which 0 were waited for; matrix products, arithmetic and copies ran while one was open for 0% of the time, Pallas kernels for 30%

profile of v2, /device:TPU:1, one launch (start us, length us, event | category | flops | bytes accessed | tf_op | source)
XLA Modules:
  0.0 56.4 jit_solution(9833986190301216764)
XLA Ops:
  0.0 0.0 copy-start
  0.0 0.0 copy-start.1
  0.0 11.1 %all-to-all-start = ((f32[64,16,128]{2,1,0:T(8,128)}), f32[64,16,128]{2,1,0:T(8,128)S(1)}, u32[]{:S(2)}, u32[]{:S(2)}) async-start(f32[64,16,128]{2,1,0:T(8,128)} %bitcast.3), calls=%async_computation | async-start | bytes 1048576 | tf_op jit(solution)/shard_map/all_to_all | solution.py:279
  11.1 0.0 copy-done
  11.1 0.0 copy-done.1
  11.1 16.9 %prepare.1 = (bf16[8,256,256]{2,1,0:T(8,128)(2,1)S(1)}, s32[9,8,128]{2,1,0:T(8,128)S(1)}, s32[4,8,128]{2,1,0:T(8,128)S(1)}) custom-call(s32[8,7]{1,0:T(8,128)S(1)} %copy-done.1, f32[8,128,128]{2,1,0:T(8,128)S(1)} %copy-done), custom_call_target="tpu_custom_call" | custom-call | flops 8000000000 | bytes 20971520 | tf_op jit(solution)/shard_map/prepare/pallas_call | solution.py:168
  28.0 0.0 all-to-all-done.x_ref
  28.0 6.0 %evolve.1 = f32[64,16,128]{2,1,0:T(8,128)S(1)} custom-call(f32[64,16,128]{2,1,0:T(8,128)S(1)} %all-to-all-done.x_ref, bf16[8,256,256]{2,1,0:T(8,128)(2,1)S(1)} %get-tuple-element.8.gates_ref, s32[9,8,128]{2,1,0:T(8,128)S(1)} %get-tuple-element.9.moves_ref, s32[4,8,128]{2,1,0:T(8,128)S(1)} %get-tuple-element.10.perms_ref), custom_call_target="tpu_custom_call" | custom-call | flops 6000000000 | bytes 20971520 | tf_op jit(solution)/shard_map/evolve/pallas_call | solution.py:259
  34.0 21.5 %all_to_all.10 = f32[64,16,128]{2,1,0:T(8,128)S(1)} all-to-all(f32[64,16,128]{2,1,0:T(8,128)S(1)} %evolve.1), channel_id=1, replica_groups=mesh['top'=2,'z'=4,'lo'=16] {'z','lo'}, dimensions={0} | all-to-all | bytes 1048576 | tf_op jit(solution)/shard_map/all_to_all | solution.py:281
  55.6 0.8 %copy.5 = f32[1,1,131072]{2,1,0:T(1,128)} copy(f32[1,1,131072]{2,1,0:T(1,128)S(1)} %bitcast.2) | data formatting | bytes 1048576
Async XLA Ops:
  0.0 11.1 %copy-start = (f32[8,128,128]{2,1,0:T(8,128)S(1)}, f32[8,128,128]{2,1,0:T(8,128)}, u32[]{:S(2)}) copy-start(f32[8,128,128]{2,1,0:T(8,128)} %stack_ref.1) | copy-start | bytes 1572868
  0.0 11.1 %copy-start.1 = (s32[8,7]{1,0:T(8,128)S(1)}, s32[8,7]{1,0:T(8,128)}, u32[]{:S(2)}) copy-start(s32[8,7]{1,0:T(8,128)} %targets_ref.1) | copy-start | bytes 676
  0.0 28.0 %all-to-all-start = ((f32[64,16,128]{2,1,0:T(8,128)}), f32[64,16,128]{2,1,0:T(8,128)S(1)}, u32[]{:S(2)}, u32[]{:S(2)}) async-start(f32[64,16,128]{2,1,0:T(8,128)} %bitcast.3), calls=%async_computation | async-start | bytes 1048576 | tf_op jit(solution)/shard_map/all_to_all | solution.py:279

commit v3 on v2

--- a/solution.py
+++ b/solution.py
@@ -34,18 +34,19 @@
     return lax.dot_general(left, right, (((1,), (0,)), ((), ())), preferred_element_type=F32)
 
 
-def left_form(value):
-    high, middle, low = three_parts(value)
+def left_form(parts):
+    high, middle, low = parts
     return jnp.concatenate([high, middle], 1), jnp.concatenate([high, low], 1)
 
 
-def right_form(value):
-    high, middle, low = three_parts(value)
+def right_form(parts):
+    high, middle, low = parts
     both = jnp.concatenate([high, middle], 1)
     return jnp.concatenate([both, both], 0), jnp.concatenate([low, high], 0)
 
 
 def full_dot(left, right):
+    left, right = left_form(left), right_form(right)
     first = dot(left[0], right[0])
     return first[:, :GATE] + (first[:, GATE:] + dot(left[1], right[1]))
 
@@ -107,7 +108,7 @@
     return position
 
 
-def prepare_kernel(targets_ref, stack_ref, gates_ref, moves_ref, perms_ref, state, gram_ref):
+def prepare_kernel(targets_ref, stack_ref, gates_ref, moves_ref, perms_ref, state, gram_ref, corners):
     lane = lax.broadcasted_iota(I32, (8, GATE), 1)
     targets, taken, left = layer_orders(targets_ref)
     for s in range(LAYERS + 1):
@@ -138,25 +139,42 @@
         deltas.append(jnp.where(out_rows == index_in[:1].astype(F32), 1.0, 0.0))
         parts = dot(jnp.concatenate(three_parts(unit), 0), jnp.concatenate([pick_in, pick_out], 1).astype(BF16))
         both = parts[:GATE] + parts[GATE : 2 * GATE] + parts[2 * GATE :]
-        ins.append(both[:, :GATE])
+        ins.append(three_parts(both[:, :GATE]))
         outs.append(both[:, GATE:].T)
-        gram_ref[g] = full_dot(left_form(both[:, :GATE]), right_form(both[:, :GATE].T))
-        state[g] = jnp.where(row == col, 2.0 / gram_ref[g], 0.0)
-
-    def level(step, carry):
-        bit = jnp.int32(1) << step
-        upper = ((row >> (step + 1)) == (col >> (step + 1))) & ((col & bit) != 0) & ((row & bit) == 0)
+        gram_ref[g] = full_dot(ins[g], three_parts(both[:, :GATE].T))
+        for part in range(4):
+            piece = gram_ref[g, 8 * part : 8 * part + 8, :]
+            for b in range(1, 4):
+                piece = jnp.where(lane >> 5 == b, gram_ref[g, 32 * b + 8 * part : 32 * b + 8 * part + 8, :], piece)
+            corners[32 * g + 8 * part : 32 * g + 8 * part + 8, :] = piece
+    solved = [None] * 32
+    for k in range(31, -1, -1):
+        entries = corners[pl.ds(k, 8, stride=32), :]
+
+        def entry(j, entries=entries):
+            return jnp.take_along_axis(entries, (lane & 96) | j, axis=1)
+
+        total = jnp.where((lane & 31) == k, 1.0, 0.0)
+        for j in range(31, k, -1):
+            total = total - entry(j) * solved[j]
+        solved[k] = total * (2.0 / entry(k))
+    for k in range(32):
+        corners[pl.ds(k, 8, stride=32), :] = solved[k]
+    for g in range(LAYERS):
+        for part in range(4):
+            piece = corners[32 * g + 8 * part : 32 * g + 8 * part + 8, :]
+            for b in range(4):
+                state[g, 32 * b + 8 * part : 32 * b + 8 * part + 8, :] = jnp.where(lane >> 5 == b, piece, 0.0)
+    for bit in (32, 64):
+        upper = ((row & -(2 * bit)) == (col & -(2 * bit))) & ((col & bit) != 0) & ((row & bit) == 0)
         for g in range(LAYERS):
-            cut = jnp.where(upper, gram_ref[g], 0.0)
             now = state[g]
-            first = full_dot(left_form(now), right_form(cut))
-            state[g] = now - full_dot(left_form(first), right_form(now))
-        return carry
-
-    lax.fori_loop(0, 7, level, 0)
+            now_parts = three_parts(now)
+            first = full_dot(now_parts, three_parts(jnp.where(upper, gram_ref[g], 0.0)))
+            state[g] = now - full_dot(three_parts(first), now_parts)
     for g in range(LAYERS):
-        inner = full_dot(left_form(state[g]), right_form(ins[g]))
-        gate = deltas[g] - full_dot(left_form(outs[g]), right_form(inner))
+        inner = full_dot(three_parts(state[g]), ins[g])
+        gate = deltas[g] - full_dot(three_parts(outs[g]), three_parts(inner))
         if g % 4 == 1:
             gate = jnp.where(row < 64, gate, pltpu.roll(gate, 64, 1))
         high, low = two_parts(gate)
@@ -177,6 +195,7 @@
         scratch_shapes=[
             pltpu.VMEM((LAYERS, GATE, GATE), F32),
             pltpu.VMEM((LAYERS, GATE, GATE), F32),
+            pltpu.VMEM((32 * LAYERS, GATE), F32),
         ],
         compiler_params=pltpu.CompilerParams(vmem_limit_bytes=24 * 2**20),
         cost_estimate=pl.CostEstimate(flops=8 * 10**9, bytes_accessed=20 * 2**20, transcendentals=0),

time: 56.6 us -> 49.7 us (0.88)
  Pallas kernels: 22.9 us -> 16.1 us
  blocking collectives: 21.5 us -> 18.8 us
  waiting for transfers between devices: 0.01 us -> 2.64 us
    pallas_call x1, Pallas kernels: 16.9 us -> 10.1 us  [prepare(): pl.pallas_call(prepare_kernel, out_shape=(jax.ShapeDtypeStruct((LAYERS, 2...]
    all_to_all x1, blocking collectives: 21.5 us -> 18.8 us  [body(): lax.all_to_all(state, group, split_axis=0, concat_axis=0, tiled=True)]
    all_to_all x1, waiting for transfers between devices: 0.01 us -> 2.64 us  [body(): lax.all_to_all(state, group, split_axis=0, concat_axis=0, tiled=True)]
  transfers between devices with their start and end apart: 1 -> 1, of which waited for: 0 -> 1; matrix products, arithmetic and copies ran while one was open for 0% -> 0% of each run, Pallas kernels for 30% -> 20%
where the time goes in v3:
time: 49.7 us; the launch traced here: 49.5 us
  blocking collectives  18.8 us (38%)
  Pallas kernels  16.1 us (32%)
  starting transfers between devices  11.1 us (22%)
  waiting for transfers between devices  2.64 us (5%)
  local copies, waits for them, and re-layouts  0.8 us (2%)
    all_to_all x1, blocking collectives, body(): lax.all_to_all(state, group, split_axis=0, concat_axis=0, tiled=True)  18.8 us
    all_to_all x1, starting transfers between devices, body(): lax.all_to_all(state, group, split_axis=0, concat_axis=0, tiled=True)  11.1 us
    pallas_call x1, Pallas kernels, prepare(): pl.pallas_call(prepare_kernel, out_shape=(jax.ShapeDtypeStruct((LAYERS, 2...  10.1 us
    pallas_call x1, Pallas kernels, evolve(): pl.pallas_call(evolve_kernel, out_shape=jax.ShapeDtypeStruct(state.shape,...  6.01 us
    all_to_all x1, waiting for transfers between devices, body(): lax.all_to_all(state, group, split_axis=0, concat_axis=0, tiled=True)  2.64 us
  transfers between devices with their start and end apart: 1, of which 1 were waited for; matrix products, arithmetic and copies ran while one was open for 0% of the time, Pallas kernels for 20%

profile of v3, /device:TPU:1, one launch (start us, length us, event | category | flops | bytes accessed | tf_op | source)
XLA Modules:
  0.0 49.5 jit_solution(2514421978926739972)
XLA Ops:
  0.0 0.0 copy-start
  0.0 0.0 copy-start.1
  0.0 11.1 %all-to-all-start = ((f32[64,16,128]{2,1,0:T(8,128)}), f32[64,16,128]{2,1,0:T(8,128)S(1)}, u32[]{:S(2)}, u32[]{:S(2)}) async-start(f32[64,16,128]{2,1,0:T(8,128)} %bitcast.3), calls=%async_computation | async-start | bytes 1048576 | tf_op jit(solution)/shard_map/all_to_all | solution.py:298
  11.1 0.0 copy-done
  11.1 0.0 copy-done.1
  11.1 10.1 %prepare.1 = (bf16[8,256,256]{2,1,0:T(8,128)(2,1)S(1)}, s32[9,8,128]{2,1,0:T(8,128)S(1)}, s32[4,8,128]{2,1,0:T(8,128)S(1)}) custom-call(s32[8,7]{1,0:T(8,128)S(1)} %copy-done.1, f32[8,128,128]{2,1,0:T(8,128)S(1)} %copy-done), custom_call_target="tpu_custom_call" | custom-call | flops 8000000000 | bytes 20971520 | tf_op jit(solution)/shard_map/prepare/pallas_call | solution.py:186
  21.2 2.6 %all-to-all-done.x_ref = f32[64,16,128]{2,1,0:T(8,128)S(1)} async-done(((f32[64,16,128]{2,1,0:T(8,128)}), f32[64,16,128]{2,1,0:T(8,128)S(1)}, u32[]{:S(2)}, u32[]{:S(2)}) %all-to-all-start) | async-done | bytes 524320 | tf_op jit(solution)/shard_map/all_to_all | solution.py:298
  23.9 6.0 %evolve.1 = f32[64,16,128]{2,1,0:T(8,128)S(1)} custom-call(f32[64,16,128]{2,1,0:T(8,128)S(1)} %all-to-all-done.x_ref, bf16[8,256,256]{2,1,0:T(8,128)(2,1)S(1)} %get-tuple-element.8.gates_ref, s32[9,8,128]{2,1,0:T(8,128)S(1)} %get-tuple-element.9.moves_ref, s32[4,8,128]{2,1,0:T(8,128)S(1)} %get-tuple-element.10.perms_ref), custom_call_target="tpu_custom_call" | custom-call | flops 6000000000 | bytes 20971520 | tf_op jit(solution)/shard_map/evolve/pallas_call | solution.py:278
  29.9 18.8 %all_to_all.10 = f32[64,16,128]{2,1,0:T(8,128)S(1)} all-to-all(f32[64,16,128]{2,1,0:T(8,128)S(1)} %evolve.1), channel_id=1, replica_groups=mesh['top'=2,'z'=4,'lo'=16] {'z','lo'}, dimensions={0} | all-to-all | bytes 1048576 | tf_op jit(solution)/shard_map/all_to_all | solution.py:300
  48.7 0.8 %copy.5 = f32[1,1,131072]{2,1,0:T(1,128)} copy(f32[1,1,131072]{2,1,0:T(1,128)S(1)} %bitcast.2) | data formatting | bytes 1048576
Async XLA Ops:
  0.0 11.1 %copy-start = (f32[8,128,128]{2,1,0:T(8,128)S(1)}, f32[8,128,128]{2,1,0:T(8,128)}, u32[]{:S(2)}) copy-start(f32[8,128,128]{2,1,0:T(8,128)} %stack_ref.1) | copy-start | bytes 1572868
  0.0 11.1 %copy-start.1 = (s32[8,7]{1,0:T(8,128)S(1)}, s32[8,7]{1,0:T(8,128)}, u32[]{:S(2)}) copy-start(s32[8,7]{1,0:T(8,128)} %targets_ref.1) | copy-start | bytes 676
  0.0 23.9 %all-to-all-start = ((f32[64,16,128]{2,1,0:T(8,128)}), f32[64,16,128]{2,1,0:T(8,128)S(1)}, u32[]{:S(2)}, u32[]{:S(2)}) async-start(f32[64,16,128]{2,1,0:T(8,128)} %bitcast.3), calls=%async_computation | async-start | bytes 1048576 | tf_op jit(solution)/shard_map/all_to_all | solution.py:298

commit v4 on v3

--- a/solution.py
+++ b/solution.py
@@ -108,19 +108,31 @@
     return position
 
 
-def prepare_kernel(targets_ref, stack_ref, gates_ref, moves_ref, perms_ref, state, gram_ref, corners):
+def prepare_kernel(targets_ref, stack_ref, gates_ref, moves_ref, picks_ref, state, gram_ref, corners):
     lane = lax.broadcasted_iota(I32, (8, GATE), 1)
     targets, taken, left = layer_orders(targets_ref)
+    shift = jnp.zeros_like(lane)
+    for m in range(1, 7):
+        shift = jnp.where(lane == 1 << m, 3 * m, shift)
     for s in range(LAYERS + 1):
         source = collect(spread(lane, taken[s + 1][3:]), left[s][3:])
-        moves_ref[s] = source * 8
+        place = jnp.zeros_like(lane)
+        for p in range(1, 7):
+            place = jnp.where(source == 1 << p, p, place)
+        code = jnp.where((lane & (lane - 1)) == 0, place << shift, 0)
+        code = jnp.sum(code.astype(F32), axis=1, keepdims=True)
+        moves_ref[pl.ds(s, 1), :] = jnp.broadcast_to(code[:1].astype(I32), (1, GATE))
     natural = [1 << m for m in range(7)]
+    perms = []
     for i, (old, new) in enumerate(
         [(natural, left[0]), (taken[4], left[4]), (taken[8], left[8]), (taken[9], natural)]
     ):
-        perms_ref[i] = collect(spread(lane, new[:7]), old[:7])
+        perms.append(collect(spread(lane, new[:7]), old[:7])[:1].astype(F32))
     row = lax.broadcasted_iota(I32, (GATE, GATE), 0)
     col = lax.broadcasted_iota(I32, (GATE, GATE), 1)
+    for i, perm in enumerate(perms):
+        perm = jnp.broadcast_to(perm, (GATE, GATE))
+        picks_ref[i] = jnp.where((perm if i == 3 else perm.T) == (row if i == 3 else col).astype(F32), 1.0, 0.0).astype(BF16)
     ins, outs, deltas = [], [], []
     for g in range(LAYERS):
         vectors = stack_ref[g]
@@ -187,8 +199,8 @@
         prepare_kernel,
         out_shape=(
             jax.ShapeDtypeStruct((LAYERS, 2 * GATE, 2 * GATE), BF16),
-            jax.ShapeDtypeStruct((LAYERS + 1, 8, GATE), I32),
-            jax.ShapeDtypeStruct((4, 8, GATE), I32),
+            jax.ShapeDtypeStruct((16, GATE), I32),
+            jax.ShapeDtypeStruct((4, GATE, GATE), BF16),
         ),
         in_specs=[pl.BlockSpec(memory_space=pltpu.SMEM), pl.BlockSpec(memory_space=pltpu.VMEM)],
         out_specs=(pl.BlockSpec(memory_space=pltpu.VMEM),) * 3,
@@ -207,23 +219,37 @@
     return jnp.concatenate([jnp.concatenate(block, 0) for block in blocks], 1)
 
 
-def evolve_kernel(x_ref, gates_ref, moves_ref, perms_ref, out_ref, here, there, table, sem):
-    copy = pltpu.make_async_copy(moves_ref, table, sem)
-    copy.start()
+def sums(steps):
+    values = [jnp.int32(0)]
+    for step in steps:
+        values += [value + step for value in values]
+    return values
+
+
+def evolve_kernel(x_ref, gates_ref, moves_ref, picks_ref, out_ref, here, there):
     lane = lax.broadcasted_iota(I32, (64, GATE), 1)
 
-    def permuted(value, i):
-        return jnp.take_along_axis(value, jnp.broadcast_to(perms_ref[i, :1, :], value.shape), axis=1)
+    def turned(pick, parts):
+        return lax.dot_general(pick, jnp.concatenate(parts, 0), (((1,), (1,)), ((), ())), preferred_element_type=F32)
+
+    def turned_sum(pick, value):
+        out = turned(pick, two_parts(value))
+        return out[:, :GATE] + out[:, GATE:]
 
     for tile in range(8):
         value = jnp.concatenate([x_ref[:, tile, :], x_ref[:, 8 + tile, :]], 0)
-        here[tile * GATE : (tile + 1) * GATE, :] = permuted(value, 0).T
-    copy.wait()
+        here[tile * GATE : (tile + 1) * GATE, :] = turned_sum(picks_ref[0], value)
+    firsts = []
+    codes = [moves_ref[stage, 0] for stage in range(LAYERS + 1)]
+    for stage in range(LAYERS + 1):
+        code = codes[stage]
+        steps = [jnp.int32(8) << ((code >> (3 * m)) & 7) for m in range(7)]
+        firsts.append((sums(steps[:4]), sums(steps[4:])))
 
     def rows(source, stage, first, count):
-        return jnp.concatenate(
-            [source[pl.ds(pl.multiple_of(table[stage, 0, first + i], 8), 8), :] for i in range(count)], 0
-        )
+        low, high = firsts[stage]
+        places = [high[(first + i) // 16] + low[(first + i) % 16] for i in range(count)]
+        return jnp.concatenate([source[pl.ds(pl.multiple_of(place, 8), 8), :] for place in places], 0)
 
     def applied(layer, blocks):
         out = dot(gates_ref[layer], side_by_side(blocks))
@@ -235,11 +261,12 @@
         if kind == 1:
             width = 16 << (layer // 4)
             one = (lane & width) != 0
+            partner = lane ^ width
             for pair in range(8):
                 blocks = []
                 for i in range(2):
                     own = rows(source, layer, (2 * pair + i) * 8, 8)
-                    other = jnp.where(one, pltpu.roll(own, width, 1), pltpu.roll(own, GATE - width, 1))
+                    other = jnp.take_along_axis(own, partner, axis=1)
                     own, other = two_parts(own), two_parts(other)
                     blocks.append([own[0], other[0], own[1], other[1]])
                 out = applied(layer, blocks)
@@ -259,17 +286,18 @@
                 value = jnp.concatenate(
                     [outs[q // 2][16 * tile : 16 * tile + 16, GATE * (q % 2) : GATE * (q % 2 + 1)] for q in range(8)], 0
                 )
-                target[tile * GATE : (tile + 1) * GATE, :] = permuted(value, 1 + layer // 4).T
+                target[tile * GATE : (tile + 1) * GATE, :] = turned_sum(picks_ref[1 + layer // 4], value)
         else:
-            for pair in range(4):
-                blocks = [two_parts(rows(source, layer, (2 * pair + i) * 16, 16)) for i in range(2)]
-                out = applied(layer, blocks)
-                for i in range(2):
-                    first = (2 * pair + i) * GATE
-                    target[first : first + GATE, :] = out[:, GATE * i : GATE * (i + 1)]
+            blocks = [two_parts(rows(source, layer, i * 16, 16)) for i in range(8)]
+            out = applied(layer, blocks)
+            for i in range(8):
+                target[i * GATE : (i + 1) * GATE, :] = out[:, GATE * i : GATE * (i + 1)]
         source, target = target, source
+    last = jnp.concatenate([picks_ref[3]] * 2, 0)
     for tile in range(8):
-        value = permuted(rows(source, LAYERS, tile * 16, 16).T, 3)
+        value = rows(source, LAYERS, tile * 16, 16).T
+        high, low = two_parts(value)
+        value = dot(jnp.concatenate([high, low], 1), last)
         out_ref[:, tile, :] = value[:64]
         out_ref[:, 8 + tile, :] = value[64:]
 
@@ -283,8 +311,6 @@
         scratch_shapes=[
             pltpu.VMEM((WIDE, GATE), F32),
             pltpu.VMEM((WIDE, GATE), F32),
-            pltpu.SMEM((LAYERS + 1, 8, GATE), I32),
-            pltpu.SemaphoreType.DMA,
         ],
         compiler_params=pltpu.CompilerParams(vmem_limit_bytes=24 * 2**20),
         cost_estimate=pl.CostEstimate(flops=6 * 10**9, bytes_accessed=20 * 2**20, transcendentals=0),

time: 49.7 us -> 48.8 us (0.982)
  Pallas kernels: 16.1 us -> 15.3 us
    pallas_call x1, Pallas kernels: 6.01 us -> 5.12 us  [evolve(): pl.pallas_call(evolve_kernel, out_shape=jax.ShapeDtypeStruct(state.shape,...]
  transfers between devices with their start and end apart: 1 -> 1, of which waited for: 1 -> 1; matrix products, arithmetic and copies ran while one was open for 0% -> 0% of each run, Pallas kernels for 20% -> 21%
where the time goes in v4:
time: 48.8 us; the launch traced here: 48.6 us
  blocking collectives  18.8 us (39%)
  Pallas kernels  15.3 us (31%)
  starting transfers between devices  11.1 us (23%)
  waiting for transfers between devices  2.6 us (5%)
  local copies, waits for them, and re-layouts  0.8 us (2%)
    all_to_all x1, blocking collectives, body(): lax.all_to_all(state, group, split_axis=0, concat_axis=0, tiled=True)  18.8 us
    all_to_all x1, starting transfers between devices, body(): lax.all_to_all(state, group, split_axis=0, concat_axis=0, tiled=True)  11.1 us
    pallas_call x1, Pallas kernels, prepare(): pl.pallas_call(prepare_kernel, out_shape=(jax.ShapeDtypeStruct((LAYERS, 2...  10.2 us
    pallas_call x1, Pallas kernels, evolve(): pl.pallas_call(evolve_kernel, out_shape=jax.ShapeDtypeStruct(state.shape,...  5.12 us
    all_to_all x1, waiting for transfers between devices, body(): lax.all_to_all(state, group, split_axis=0, concat_axis=0, tiled=True)  2.6 us
  transfers between devices with their start and end apart: 1, of which 1 were waited for; matrix products, arithmetic and copies ran while one was open for 0% of the time, Pallas kernels for 21%

profile of v4, /device:TPU:1, one launch (start us, length us, event | category | flops | bytes accessed | tf_op | source)
XLA Modules:
  0.0 48.6 jit_solution(3642936510045552674)
XLA Ops:
  0.0 0.0 copy-start
  0.0 0.0 copy-start.1
  0.0 11.1 %all-to-all-start = ((f32[64,16,128]{2,1,0:T(8,128)}), f32[64,16,128]{2,1,0:T(8,128)S(1)}, u32[]{:S(2)}, u32[]{:S(2)}) async-start(f32[64,16,128]{2,1,0:T(8,128)} %bitcast.3), calls=%async_computation | async-start | bytes 1048576 | tf_op jit(solution)/shard_map/all_to_all | solution.py:324
  11.1 0.0 copy-done
  11.1 0.0 copy-done.1
  11.1 10.2 %prepare.1 = (bf16[8,256,256]{2,1,0:T(8,128)(2,1)S(1)}, s32[16,128]{1,0:T(8,128)S(1)}, bf16[4,128,128]{2,1,0:T(8,128)(2,1)S(1)}) custom-call(s32[8,7]{1,0:T(8,128)S(1)} %copy-done.1, f32[8,128,128]{2,1,0:T(8,128)S(1)} %copy-done), custom_call_target="tpu_custom_call" | custom-call | flops 8000000000 | bytes 20971520 | tf_op jit(solution)/shard_map/prepare/pallas_call | solution.py:198
  21.3 2.6 %all-to-all-done.x_ref = f32[64,16,128]{2,1,0:T(8,128)S(1)} async-done(((f32[64,16,128]{2,1,0:T(8,128)}), f32[64,16,128]{2,1,0:T(8,128)S(1)}, u32[]{:S(2)}, u32[]{:S(2)}) %all-to-all-start) | async-done | bytes 524320 | tf_op jit(solution)/shard_map/all_to_all | solution.py:324
  23.9 5.1 %evolve.1 = f32[64,16,128]{2,1,0:T(8,128)S(1)} custom-call(f32[64,16,128]{2,1,0:T(8,128)S(1)} %all-to-all-done.x_ref, bf16[8,256,256]{2,1,0:T(8,128)(2,1)S(1)} %get-tuple-element.8.gates_ref, s32[16,128]{1,0:T(8,128)S(1)} %get-tuple-element.9.moves_ref, bf16[4,128,128]{2,1,0:T(8,128)(2,1)S(1)} %get-tuple-element.10.picks_ref), custom_call_target="tpu_custom_call" | custom-call | flops 6000000000 | bytes 20971520 | tf_op jit(solution)/shard_map/evolve/pallas_call | solution.py:306
  29.0 18.8 %all_to_all.10 = f32[64,16,128]{2,1,0:T(8,128)S(1)} all-to-all(f32[64,16,128]{2,1,0:T(8,128)S(1)} %evolve.1), channel_id=1, replica_groups=mesh['top'=2,'z'=4,'lo'=16] {'z','lo'}, dimensions={0} | all-to-all | bytes 1048576 | tf_op jit(solution)/shard_map/all_to_all | solution.py:326
  47.8 0.8 %copy.5 = f32[1,1,131072]{2,1,0:T(1,128)} copy(f32[1,1,131072]{2,1,0:T(1,128)S(1)} %bitcast.2) | data formatting | bytes 1048576
Async XLA Ops:
  0.0 11.1 %copy-start = (f32[8,128,128]{2,1,0:T(8,128)S(1)}, f32[8,128,128]{2,1,0:T(8,128)}, u32[]{:S(2)}) copy-start(f32[8,128,128]{2,1,0:T(8,128)} %stack_ref.1) | copy-start | bytes 1572868
  0.0 11.1 %copy-start.1 = (s32[8,7]{1,0:T(8,128)S(1)}, s32[8,7]{1,0:T(8,128)}, u32[]{:S(2)}) copy-start(s32[8,7]{1,0:T(8,128)} %targets_ref.1) | copy-start | bytes 676
  0.0 23.9 %all-to-all-start = ((f32[64,16,128]{2,1,0:T(8,128)}), f32[64,16,128]{2,1,0:T(8,128)S(1)}, u32[]{:S(2)}, u32[]{:S(2)}) async-start(f32[64,16,128]{2,1,0:T(8,128)} %bitcast.3), calls=%async_computation | async-start | bytes 1048576 | tf_op jit(solution)/shard_map/all_to_all | solution.py:324

commit v5 on v4

--- a/solution.py
+++ b/solution.py
@@ -133,11 +133,9 @@
     for i, perm in enumerate(perms):
         perm = jnp.broadcast_to(perm, (GATE, GATE))
         picks_ref[i] = jnp.where((perm if i == 3 else perm.T) == (row if i == 3 else col).astype(F32), 1.0, 0.0).astype(BF16)
-    ins, outs, deltas = [], [], []
-    for g in range(LAYERS):
-        vectors = stack_ref[g]
-        lengths = jnp.sum(vectors * vectors, axis=1, keepdims=True)
-        unit = vectors * lax.rsqrt(lengths)
+    tall = lax.broadcasted_iota(I32, (2 * GATE, GATE), 0)
+    picks_in, picks_out = [], []
+    for g in range(LAYERS):
         if g % 4 == 3:
             index_in = index_out = (lane & 15) << 3 | lane >> 4
         else:
@@ -145,15 +143,16 @@
             index_in, index_out = (
                 collect(spread(lane, order[g + 1][:count]), targets[g]) + (lane >> count << count) for order in (taken, left)
             )
-        pick_in = jnp.where(row == index_in[:1], 1.0, 0.0)
-        pick_out = jnp.where(row == index_out[:1], 1.0, 0.0)
-        out_rows = jnp.broadcast_to(index_out[:1], (GATE, GATE)).astype(F32).T
-        deltas.append(jnp.where(out_rows == index_in[:1].astype(F32), 1.0, 0.0))
-        parts = dot(jnp.concatenate(three_parts(unit), 0), jnp.concatenate([pick_in, pick_out], 1).astype(BF16))
-        both = parts[:GATE] + parts[GATE : 2 * GATE] + parts[2 * GATE :]
-        ins.append(three_parts(both[:, :GATE]))
-        outs.append(both[:, GATE:].T)
-        gram_ref[g] = full_dot(ins[g], three_parts(both[:, :GATE].T))
+        picks_in.append(jnp.where(row == index_in[:1], 1.0, 0.0).astype(BF16))
+        picks_out.append(jnp.where(row == index_out[:1], 1.0, 0.0).T.astype(BF16))
+    units, units_t = [], []
+    for g in range(LAYERS):
+        vectors = stack_ref[g]
+        lengths = jnp.sum(vectors * vectors, axis=1, keepdims=True)
+        unit = vectors * lax.rsqrt(lengths)
+        units.append(three_parts(unit))
+        units_t.append(three_parts(unit.T))
+        gram_ref[g] = full_dot(units[g], units_t[g])
         for part in range(4):
             piece = gram_ref[g, 8 * part : 8 * part + 8, :]
             for b in range(1, 4):
@@ -179,19 +178,28 @@
                 state[g, 32 * b + 8 * part : 32 * b + 8 * part + 8, :] = jnp.where(lane >> 5 == b, piece, 0.0)
     for bit in (32, 64):
         upper = ((row & -(2 * bit)) == (col & -(2 * bit))) & ((col & bit) != 0) & ((row & bit) == 0)
+        halves = [slice(first, first + bit) for first in range(0, GATE, 2 * bit)]
+        firsts = []
         for g in range(LAYERS):
-            now = state[g]
-            now_parts = three_parts(now)
-            first = full_dot(now_parts, three_parts(jnp.where(upper, gram_ref[g], 0.0)))
-            state[g] = now - full_dot(three_parts(first), now_parts)
-    for g in range(LAYERS):
-        inner = full_dot(three_parts(state[g]), ins[g])
-        gate = deltas[g] - full_dot(three_parts(outs[g]), three_parts(inner))
+            top = jnp.concatenate([state[g, half, :] for half in halves], 0)
+            firsts.append(full_dot(three_parts(top), three_parts(jnp.where(upper, gram_ref[g], 0.0))))
+        for g in range(LAYERS):
+            change = full_dot(three_parts(firsts[g]), three_parts(state[g]))
+            for i, half in enumerate(halves):
+                state[g, half, :] = state[g, half, :] - change[bit * i : bit * (i + 1)]
+    inners = [full_dot(three_parts(state[g]), units[g]) for g in range(LAYERS)]
+    gates = [
+        jnp.where(row == col, 1.0, 0.0) - full_dot(units_t[g], three_parts(inners[g])) for g in range(LAYERS)
+    ]
+    moved = []
+    for g in range(LAYERS):
+        moved.append(dot(picks_out[g], jnp.concatenate(two_parts(gates[g]), 1)).astype(BF16))
+    for g in range(LAYERS):
+        parts = dot(jnp.concatenate([moved[g][:, :GATE], moved[g][:, GATE:]], 0), picks_in[g])
         if g % 4 == 1:
-            gate = jnp.where(row < 64, gate, pltpu.roll(gate, 64, 1))
-        high, low = two_parts(gate)
-        gates_ref[g, :GATE, :] = jnp.concatenate([high, high], 1)
-        gates_ref[g, GATE:, :] = jnp.concatenate([low, low], 1)
+            parts = jnp.where((tall & 64) == 0, parts, pltpu.roll(parts, 64, 1))
+        parts = parts.astype(BF16)
+        gates_ref[g] = jnp.concatenate([parts, parts], 1)
 
 
 def prepare(targets, gate_stack):
@@ -236,9 +244,10 @@
         out = turned(pick, two_parts(value))
         return out[:, :GATE] + out[:, GATE:]
 
+    values = [jnp.concatenate([x_ref[:, tile, :], x_ref[:, 8 + tile, :]], 0) for tile in range(8)]
+    values = [turned_sum(picks_ref[0], value) for value in values]
     for tile in range(8):
-        value = jnp.concatenate([x_ref[:, tile, :], x_ref[:, 8 + tile, :]], 0)
-        here[tile * GATE : (tile + 1) * GATE, :] = turned_sum(picks_ref[0], value)
+        here[tile * GATE : (tile + 1) * GATE, :] = values[tile]
     firsts = []
     codes = [moves_ref[stage, 0] for stage in range(LAYERS + 1)]
     for stage in range(LAYERS + 1):
@@ -262,31 +271,33 @@
             width = 16 << (layer // 4)
             one = (lane & width) != 0
             partner = lane ^ width
-            for pair in range(8):
-                blocks = []
-                for i in range(2):
-                    own = rows(source, layer, (2 * pair + i) * 8, 8)
-                    other = jnp.take_along_axis(own, partner, axis=1)
-                    own, other = two_parts(own), two_parts(other)
-                    blocks.append([own[0], other[0], own[1], other[1]])
-                out = applied(layer, blocks)
-                for i in range(2):
-                    first = (2 * pair + i) * 64
-                    part = out[:, GATE * i : GATE * (i + 1)]
-                    target[first : first + 64, :] = jnp.where(one, part[64:], part[:64])
+            blocks = []
+            for i in range(16):
+                own = rows(source, layer, i * 8, 8)
+                other = jnp.take_along_axis(own, partner, axis=1)
+                own, other = two_parts(own), two_parts(other)
+                blocks.append([own[0], other[0], own[1], other[1]])
+            out = applied(layer, blocks)
+            for i in range(16):
+                part = out[:, GATE * i : GATE * (i + 1)]
+                target[i * 64 : (i + 1) * 64, :] = jnp.where(one, part[64:], part[:64])
         elif kind == 3:
-            tiles = [two_parts(rows(source, layer, tile * 16, 16).T) for tile in range(8)]
+            tiles = [rows(source, layer, tile * 16, 16) for tile in range(8)]
+            tiles = [two_parts(tile.T) for tile in tiles]
             outs = []
             for q in range(0, 8, 2):
                 blocks = [
                     [tiles[t][part][16 * p : 16 * p + 16] for part in range(2) for t in range(8)] for p in (q, q + 1)
                 ]
                 outs.append(applied(layer, blocks))
+            values = []
             for tile in range(8):
                 value = jnp.concatenate(
                     [outs[q // 2][16 * tile : 16 * tile + 16, GATE * (q % 2) : GATE * (q % 2 + 1)] for q in range(8)], 0
                 )
-                target[tile * GATE : (tile + 1) * GATE, :] = turned_sum(picks_ref[1 + layer // 4], value)
+                values.append(turned_sum(picks_ref[1 + layer // 4], value))
+            for tile in range(8):
+                target[tile * GATE : (tile + 1) * GATE, :] = values[tile]
         else:
             blocks = [two_parts(rows(source, layer, i * 16, 16)) for i in range(8)]
             out = applied(layer, blocks)
@@ -294,12 +305,11 @@
                 target[i * GATE : (i + 1) * GATE, :] = out[:, GATE * i : GATE * (i + 1)]
         source, target = target, source
     last = jnp.concatenate([picks_ref[3]] * 2, 0)
+    values = [rows(source, LAYERS, tile * 16, 16) for tile in range(8)]
+    values = [dot(jnp.concatenate(two_parts(value.T), 1), last) for value in values]
     for tile in range(8):
-        value = rows(source, LAYERS, tile * 16, 16).T
-        high, low = two_parts(value)
-        value = dot(jnp.concatenate([high, low], 1), last)
-        out_ref[:, tile, :] = value[:64]
-        out_ref[:, 8 + tile, :] = value[64:]
+        out_ref[:, tile, :] = values[tile][:64]
+        out_ref[:, 8 + tile, :] = values[tile][64:]
 
 
 def evolve(state, gates, moves, perms):

time: 48.8 us -> 46.9 us (0.961)
  Pallas kernels: 15.3 us -> 10.1 us
  waiting for transfers between devices: 2.6 us -> 7.79 us
  blocking collectives: 18.8 us -> 16.9 us
    all_to_all x1, waiting for transfers between devices: 2.6 us -> 7.79 us  [body(): lax.all_to_all(state, group, split_axis=0, concat_axis=0, tiled=True)]
    pallas_call x1, Pallas kernels: 10.2 us -> 4.98 us  [prepare(): pl.pallas_call(prepare_kernel, out_shape=(jax.ShapeDtypeStruct((LAYERS, 2...]
    all_to_all x1, blocking collectives: 18.8 us -> 16.9 us  [body(): lax.all_to_all(state, group, split_axis=0, concat_axis=0, tiled=True)]
  transfers between devices with their start and end apart: 1 -> 1, of which waited for: 1 -> 1; matrix products, arithmetic and copies ran while one was open for 0% -> 0% of each run, Pallas kernels for 21% -> 11%
where the time goes in v5:
time: 46.9 us; the launch traced here: 46.6 us
  blocking collectives  16.9 us (36%)
  starting transfers between devices  11.1 us (24%)
  Pallas kernels  10.1 us (22%)
  waiting for transfers between devices  7.79 us (17%)
  local copies, waits for them, and re-layouts  0.8 us (2%)
    all_to_all x1, blocking collectives, body(): lax.all_to_all(state, group, split_axis=0, concat_axis=0, tiled=True)  16.9 us
    all_to_all x1, starting transfers between devices, body(): lax.all_to_all(state, group, split_axis=0, concat_axis=0, tiled=True)  11.1 us
    all_to_all x1, waiting for transfers between devices, body(): lax.all_to_all(state, group, split_axis=0, concat_axis=0, tiled=True)  7.79 us
    pallas_call x1, Pallas kernels, evolve(): pl.pallas_call(evolve_kernel, out_shape=jax.ShapeDtypeStruct(state.shape,...  5.08 us
    pallas_call x1, Pallas kernels, prepare(): pl.pallas_call(prepare_kernel, out_shape=(jax.ShapeDtypeStruct((LAYERS, 2...  4.98 us
  transfers between devices with their start and end apart: 1, of which 1 were waited for; matrix products, arithmetic and copies ran while one was open for 0% of the time, Pallas kernels for 11%

profile of v5, /device:TPU:1, one launch (start us, length us, event | category | flops | bytes accessed | tf_op | source)
XLA Modules:
  0.0 46.6 jit_solution(15986208512624427969)
XLA Ops:
  0.0 0.0 copy-start
  0.0 0.0 copy-start.1
  0.0 11.1 %all-to-all-start = ((f32[64,16,128]{2,1,0:T(8,128)}), f32[64,16,128]{2,1,0:T(8,128)S(1)}, u32[]{:S(2)}, u32[]{:S(2)}) async-start(f32[64,16,128]{2,1,0:T(8,128)} %bitcast.3), calls=%async_computation | async-start | bytes 1048576 | tf_op jit(solution)/shard_map/all_to_all | solution.py:334
  11.1 0.0 copy-done
  11.1 0.0 copy-done.1
  11.1 5.0 %prepare.1 = (bf16[8,256,256]{2,1,0:T(8,128)(2,1)S(1)}, s32[16,128]{1,0:T(8,128)S(1)}, bf16[4,128,128]{2,1,0:T(8,128)(2,1)S(1)}) custom-call(s32[8,7]{1,0:T(8,128)S(1)} %copy-done.1, f32[8,128,128]{2,1,0:T(8,128)S(1)} %copy-done), custom_call_target="tpu_custom_call" | custom-call | flops 8000000000 | bytes 20971520 | tf_op jit(solution)/shard_map/prepare/pallas_call | solution.py:206
  16.1 7.8 %all-to-all-done.x_ref = f32[64,16,128]{2,1,0:T(8,128)S(1)} async-done(((f32[64,16,128]{2,1,0:T(8,128)}), f32[64,16,128]{2,1,0:T(8,128)S(1)}, u32[]{:S(2)}, u32[]{:S(2)}) %all-to-all-start) | async-done | bytes 524320 | tf_op jit(solution)/shard_map/all_to_all | solution.py:334
  23.9 5.1 %evolve.1 = f32[64,16,128]{2,1,0:T(8,128)S(1)} custom-call(f32[64,16,128]{2,1,0:T(8,128)S(1)} %all-to-all-done.x_ref, bf16[8,256,256]{2,1,0:T(8,128)(2,1)S(1)} %get-tuple-element.8.gates_ref, s32[16,128]{1,0:T(8,128)S(1)} %get-tuple-element.9.moves_ref, bf16[4,128,128]{2,1,0:T(8,128)(2,1)S(1)} %get-tuple-element.10.picks_ref), custom_call_target="tpu_custom_call" | custom-call | flops 6000000000 | bytes 20971520 | tf_op jit(solution)/shard_map/evolve/pallas_call | solution.py:316
  29.0 16.9 %all_to_all.10 = f32[64,16,128]{2,1,0:T(8,128)S(1)} all-to-all(f32[64,16,128]{2,1,0:T(8,128)S(1)} %evolve.1), channel_id=1, replica_groups=mesh['top'=2,'z'=4,'lo'=16] {'z','lo'}, dimensions={0} | all-to-all | bytes 1048576 | tf_op jit(solution)/shard_map/all_to_all | solution.py:336
  45.9 0.8 %copy.5 = f32[1,1,131072]{2,1,0:T(1,128)} copy(f32[1,1,131072]{2,1,0:T(1,128)S(1)} %bitcast.2) | data formatting | bytes 1048576
Async XLA Ops:
  0.0 11.1 %copy-start = (f32[8,128,128]{2,1,0:T(8,128)S(1)}, f32[8,128,128]{2,1,0:T(8,128)}, u32[]{:S(2)}) copy-start(f32[8,128,128]{2,1,0:T(8,128)} %stack_ref.1) | copy-start | bytes 1572868
  0.0 11.1 %copy-start.1 = (s32[8,7]{1,0:T(8,128)S(1)}, s32[8,7]{1,0:T(8,128)}, u32[]{:S(2)}) copy-start(s32[8,7]{1,0:T(8,128)} %targets_ref.1) | copy-start | bytes 676
  0.0 23.9 %all-to-all-start = ((f32[64,16,128]{2,1,0:T(8,128)}), f32[64,16,128]{2,1,0:T(8,128)S(1)}, u32[]{:S(2)}, u32[]{:S(2)}) async-start(f32[64,16,128]{2,1,0:T(8,128)} %bitcast.3), calls=%async_computation | async-start | bytes 1048576 | tf_op jit(solution)/shard_map/all_to_all | solution.py:334

commit v6 on v5

--- a/solution.py
+++ b/solution.py
@@ -234,7 +234,7 @@
     return values
 
 
-def evolve_kernel(x_ref, gates_ref, moves_ref, picks_ref, out_ref, here, there):
+def evolve_kernel(core_ref, x_ref, gates_ref, moves_ref, picks_ref, out_ref, send_ref, here, there, ends):
     lane = lax.broadcasted_iota(I32, (64, GATE), 1)
 
     def turned(pick, parts):
@@ -308,37 +308,46 @@
     values = [rows(source, LAYERS, tile * 16, 16) for tile in range(8)]
     values = [dot(jnp.concatenate(two_parts(value.T), 1), last) for value in values]
     for tile in range(8):
-        out_ref[:, tile, :] = values[tile][:64]
-        out_ref[:, 8 + tile, :] = values[tile][64:]
-
-
-def evolve(state, gates, moves, perms):
+        ends[:, tile, :] = values[tile][:64]
+        ends[:, 8 + tile, :] = values[tile][64:]
+    core = core_ref[0]
+    for pair in range(32):
+        out_ref[pair, core] = ends[2 * pair + core]
+        send_ref[pair] = ends[2 * pair + 1 - core]
+
+
+def evolve(core, state, gates, moves, perms):
     return pl.pallas_call(
         evolve_kernel,
-        out_shape=jax.ShapeDtypeStruct(state.shape, F32),
-        in_specs=[pl.BlockSpec(memory_space=pltpu.VMEM)] * 4,
-        out_specs=pl.BlockSpec(memory_space=pltpu.VMEM),
+        out_shape=(
+            jax.ShapeDtypeStruct((32, 2, 16, GATE), F32),
+            jax.ShapeDtypeStruct((32, 16, GATE), F32),
+        ),
+        in_specs=[pl.BlockSpec(memory_space=pltpu.SMEM)] + [pl.BlockSpec(memory_space=pltpu.VMEM)] * 4,
+        out_specs=(pl.BlockSpec(memory_space=pltpu.VMEM),) * 2,
         scratch_shapes=[
             pltpu.VMEM((WIDE, GATE), F32),
             pltpu.VMEM((WIDE, GATE), F32),
+            pltpu.VMEM((64, 16, GATE), F32),
         ],
         compiler_params=pltpu.CompilerParams(vmem_limit_bytes=24 * 2**20),
         cost_estimate=pl.CostEstimate(flops=6 * 10**9, bytes_accessed=20 * 2**20, transcendentals=0),
         name="evolve",
-    )(state, gates, moves, perms)
+    )(core, state, gates, moves, perms)
 
 
 def body(amplitudes, gate_stack, targets):
-    group = ("z", "lo")
+    core = lax.axis_index("core").astype(I32)
     state = amplitudes.reshape(64, 16, 128)
-    state = lax.all_to_all(state, group, split_axis=0, concat_axis=0, tiled=True)
-    state = evolve(state, *prepare(targets, gate_stack))
-    state = lax.all_to_all(state, group, split_axis=0, concat_axis=0, tiled=True)
+    state = lax.all_to_all(state, ("z", "yx", "core"), split_axis=0, concat_axis=0, tiled=True)
+    kept, sent = evolve(core[None], state, *prepare(targets, gate_stack))
+    got = lax.ppermute(sent, "core", [(0, 1), (1, 0)])
+    state = lax.dynamic_update_slice_in_dim(kept, got[:, None], 1 - core, 1)
+    state = lax.all_to_all(state, ("z", "yx"), split_axis=0, concat_axis=0, tiled=True)
     return state.reshape(amplitudes.shape)
 
 
 def solution(mesh):
-    split = Mesh(mesh.devices.reshape(2, 4, 16), ("top", "z", "lo"))
-    in_specs = (P(("top", "z"), "lo", None), P(), P())
-    out_specs = P(("top", "z"), "lo", None)
-    return jax.shard_map(body, mesh=split, in_specs=in_specs, out_specs=out_specs, check_vma=False)
+    split = Mesh(mesh.devices.reshape(2, 4, 8, 2), ("top", "z", "yx", "core"))
+    place = P(("top", "z"), ("yx", "core"), None)
+    return jax.shard_map(body, mesh=split, in_specs=(place, P(), P()), out_specs=place, check_vma=False)

time: 46.9 us -> 46.8 us (level)
  blocking collectives: 16.9 us -> 14.6 us
  local copies, waits for them, and re-layouts: 0.8 us -> 1.49 us
  starting transfers between devices: 11.1 us -> 11.6 us
  waiting for transfers between devices: 7.79 us -> 8.29 us
    all_to_all x1, blocking collectives: 16.9 us -> 14.6 us  [body(): lax.all_to_all(state, ('z', 'yx'), split_axis=0, concat_axis=0, tiled=True)]
    ppermute x0 -> x1, waiting for transfers between devices: none -> 1.16 us  [body(): got = lax.ppermute(sent, 'core', [(0, 1), (1, 0)])]
    all_to_all x1, waiting for transfers between devices: 7.79 us -> 7.13 us  [body(): lax.all_to_all(state, ('z', 'yx', 'core'), split_axis=0, concat_axis=0, t...]
    unnamed x5, local copies, waits for them, and re-layouts: 0.8 us -> 1.46 us
    ppermute x0 -> x1, starting transfers between devices: none -> 0.55 us  [body(): got = lax.ppermute(sent, 'core', [(0, 1), (1, 0)])]
  transfers between devices with their start and end apart: 1 -> 2, of which waited for: 1 -> 2; matrix products, arithmetic and copies ran while one was open for 0% -> 0% of each run, Pallas kernels for 11% -> 11%
where the time goes in v6:
time: 46.8 us; the launch traced here: 46.1 us
  blocking collectives  14.6 us (31%)
  starting transfers between devices  11.6 us (25%)
  Pallas kernels  10.1 us (22%)
  waiting for transfers between devices  8.29 us (18%)
  local copies, waits for them, and re-layouts  1.49 us (3%)
    all_to_all x1, blocking collectives, body(): lax.all_to_all(state, ('z', 'yx'), split_axis=0, concat_axis=0, tiled=True)  14.6 us
    all_to_all x1, starting transfers between devices, body(): lax.all_to_all(state, ('z', 'yx', 'core'), split_axis=0, concat_axis=0, t...  11.1 us
    all_to_all x1, waiting for transfers between devices, body(): lax.all_to_all(state, ('z', 'yx', 'core'), split_axis=0, concat_axis=0, t...  7.13 us
    pallas_call x1, Pallas kernels, evolve(): pl.pallas_call(evolve_kernel, out_shape=(jax.ShapeDtypeStruct((32, 2, 16,...  5.12 us
    pallas_call x1, Pallas kernels, prepare(): pl.pallas_call(prepare_kernel, out_shape=(jax.ShapeDtypeStruct((LAYERS, 2...  4.97 us
    unnamed x5, local copies, waits for them, and re-layouts  1.46 us
    ppermute x1, waiting for transfers between devices, body(): got = lax.ppermute(sent, 'core', [(0, 1), (1, 0)])  1.16 us
  transfers between devices with their start and end apart: 2, of which 2 were waited for; matrix products, arithmetic and copies ran while one was open for 0% of the time, Pallas kernels for 11%

profile of v6, /device:TPU:1, one launch (start us, length us, event | category | flops | bytes accessed | tf_op | source)
XLA Modules:
  0.0 46.1 jit_solution(12269452298750248011)
XLA Ops:
  0.0 0.0 copy-start
  0.0 11.1 %all-to-all-start = ((f32[64,16,128]{2,1,0:T(8,128)}), f32[64,16,128]{2,1,0:T(8,128)S(1)}, u32[]{:S(2)}, u32[]{:S(2)}) async-start(f32[64,16,128]{2,1,0:T(8,128)} %bitcast.8), calls=%async_computation | async-start | bytes 1048576 | tf_op jit(solution)/shard_map/all_to_all | solution.py:342
  11.1 0.0 copy-start.1
  11.1 0.0 copy-done
  11.1 0.7 %copy-done.1 = s32[8,7]{1,0:T(8,128)S(1)} copy-done((s32[8,7]{1,0:T(8,128)S(1)}, s32[8,7]{1,0:T(8,128)}, u32[]{:S(2)}) %copy-start.1) | copy-done | bytes 248
  11.8 5.0 %prepare.1 = (bf16[8,256,256]{2,1,0:T(8,128)(2,1)S(1)}, s32[16,128]{1,0:T(8,128)S(1)}, bf16[4,128,128]{2,1,0:T(8,128)(2,1)S(1)}) custom-call(s32[8,7]{1,0:T(8,128)S(1)} %copy-done.1, f32[8,128,128]{2,1,0:T(8,128)S(1)} %copy-done), custom_call_target="tpu_custom_call" | custom-call | flops 8000000000 | bytes 20971520 | tf_op jit(solution)/shard_map/prepare/pallas_call | solution.py:206
  16.7 7.1 %all-to-all-done.x_ref = f32[64,16,128]{2,1,0:T(8,128)S(1)} async-done(((f32[64,16,128]{2,1,0:T(8,128)}), f32[64,16,128]{2,1,0:T(8,128)S(1)}, u32[]{:S(2)}, u32[]{:S(2)}) %all-to-all-start) | async-done | bytes 524320 | tf_op jit(solution)/shard_map/all_to_all | solution.py:342
  23.9 5.1 %evolve.1 = (f32[32,2,16,128]{3,2,1,0:T(8,128)S(1)}, f32[32,16,128]{2,1,0:T(8,128)S(1)}) custom-call(s32[1]{0:T(128)} %bitcast.core_ref, f32[64,16,128]{2,1,0:T(8,128)S(1)} %all-to-all-done.x_ref, bf16[8,256,256]{2,1,0:T(8,128)(2,1)S(1)} %get-tuple-element.10.gates_ref, s32[16,128]{1,0:T(8,128)S(1)} %get-tuple-element.11.moves_ref, ...), custom_call_target="tpu_custom_call" | custom-call | flops 6000000000 | bytes 20971520 | tf_op jit(solution)/shard_map/evolve/pallas_call | solution.py:320
  29.0 0.6 %collective-permute-start = (f32[32,16,128]{2,1,0:T(8,128)S(1)}, f32[32,16,128]{2,1,0:T(8,128)S(1)}, u32[]{:S(2)}, u32[]{:S(2)}) collective-permute-start(f32[32,16,128]{2,1,0:T(8,128)S(1)} %get-tuple-element.14), channel_id=1, source_target_pairs={{0,1},{1,0},{2,3},{3,2},{4,5},{5,4},{6,7},{7,6},{8,9},{9,8},{10,11... | collective-permute-start | bytes 786440 | tf_op jit(solution)/shard_map/ppermute | solution.py:344
  29.5 1.2 %collective-permute-done = f32[32,16,128]{2,1,0:T(8,128)S(1)} collective-permute-done((f32[32,16,128]{2,1,0:T(8,128)S(1)}, f32[32,16,128]{2,1,0:T(8,128)S(1)}, u32[]{:S(2)}, u32[]{:S(2)}) %collective-permute-start) | collective-permute-done | bytes 262176 | tf_op jit(solution)/shard_map/ppermute | solution.py:344
  30.7 14.6 %all_to_all.10 = f32[32,2,16,128]{3,2,1,0:T(8,128)S(1)} all-to-all(f32[32,2,16,128]{3,2,1,0:T(8,128)S(1)} %bitcast_dynamic-update-slice_fusion), channel_id=1, replica_groups=mesh['top'=2,'z'=4,'yx'=8,'core'=2] {'z','yx'}, dimensions={0} | all-to-all | bytes 1048576 | tf_op jit(solution)/shard_map/all_to_all | solution.py:346
  45.3 0.8 %copy.7 = f32[1,1,131072]{2,1,0:T(1,128)} copy(f32[1,1,131072]{2,1,0:T(1,128)S(1)} %bitcast.7) | data formatting | bytes 1048576
  (1 shorter events, 0.0 us)
Async XLA Ops:
  0.0 11.1 %copy-start = (f32[8,128,128]{2,1,0:T(8,128)S(1)}, f32[8,128,128]{2,1,0:T(8,128)}, u32[]{:S(2)}) copy-start(f32[8,128,128]{2,1,0:T(8,128)} %stack_ref.1) | copy-start | bytes 1572868
  0.0 23.9 %all-to-all-start = ((f32[64,16,128]{2,1,0:T(8,128)}), f32[64,16,128]{2,1,0:T(8,128)S(1)}, u32[]{:S(2)}, u32[]{:S(2)}) async-start(f32[64,16,128]{2,1,0:T(8,128)} %bitcast.8), calls=%async_computation | async-start | bytes 1048576 | tf_op jit(solution)/shard_map/all_to_all | solution.py:342
  11.1 0.7 %copy-start.1 = (s32[8,7]{1,0:T(8,128)S(1)}, s32[8,7]{1,0:T(8,128)}, u32[]{:S(2)}) copy-start(s32[8,7]{1,0:T(8,128)} %targets_ref.1) | copy-start | bytes 676
  29.0 1.7 %collective-permute-start = (f32[32,16,128]{2,1,0:T(8,128)S(1)}, f32[32,16,128]{2,1,0:T(8,128)S(1)}, u32[]{:S(2)}, u32[]{:S(2)}) collective-permute-start(f32[32,16,128]{2,1,0:T(8,128)S(1)} %get-tuple-element.14), channel_id=1, source_target_pairs={{0,1},{1,0},{2,3},{3,2},{4,5},{5,4},{6,7},{7,6},{8,9},{9,8},{10,11... | collective-permute-start | bytes 786440 | tf_op jit(solution)/shard_map/ppermute | solution.py:344

commit v7 on v6

--- a/solution.py
+++ b/solution.py
@@ -199,14 +199,14 @@
         if g % 4 == 1:
             parts = jnp.where((tall & 64) == 0, parts, pltpu.roll(parts, 64, 1))
         parts = parts.astype(BF16)
-        gates_ref[g] = jnp.concatenate([parts, parts], 1)
+        gates_ref[g] = jnp.concatenate([parts[:GATE], parts[:GATE], parts[GATE:]], 1)
 
 
 def prepare(targets, gate_stack):
     return pl.pallas_call(
         prepare_kernel,
         out_shape=(
-            jax.ShapeDtypeStruct((LAYERS, 2 * GATE, 2 * GATE), BF16),
+            jax.ShapeDtypeStruct((LAYERS, GATE, 3 * GATE), BF16),
             jax.ShapeDtypeStruct((16, GATE), I32),
             jax.ShapeDtypeStruct((4, GATE, GATE), BF16),
         ),
@@ -237,12 +237,13 @@
 def evolve_kernel(core_ref, x_ref, gates_ref, moves_ref, picks_ref, out_ref, send_ref, here, there, ends):
     lane = lax.broadcasted_iota(I32, (64, GATE), 1)
 
-    def turned(pick, parts):
-        return lax.dot_general(pick, jnp.concatenate(parts, 0), (((1,), (1,)), ((), ())), preferred_element_type=F32)
-
     def turned_sum(pick, value):
-        out = turned(pick, two_parts(value))
-        return out[:, :GATE] + out[:, GATE:]
+        return lax.dot_general(
+            jnp.concatenate([pick, pick], 1),
+            jnp.concatenate(two_parts(value), 1),
+            (((1,), (1,)), ((), ())),
+            preferred_element_type=F32,
+        )
 
     values = [jnp.concatenate([x_ref[:, tile, :], x_ref[:, 8 + tile, :]], 0) for tile in range(8)]
     values = [turned_sum(picks_ref[0], value) for value in values]
@@ -261,8 +262,8 @@
         return jnp.concatenate([source[pl.ds(pl.multiple_of(place, 8), 8), :] for place in places], 0)
 
     def applied(layer, blocks):
-        out = dot(gates_ref[layer], side_by_side(blocks))
-        return out[:GATE] + out[GATE:]
+        stacked = side_by_side(blocks)
+        return dot(gates_ref[layer], jnp.concatenate([stacked, stacked[:GATE]], 0))
 
     source, target = here, there
     for layer in range(LAYERS):

time: 46.8 us -> 46.7 us (level)
  no operation moved by 1% of the time
where the time goes in v7:
time: 46.7 us; the launch traced here: 46 us
  blocking collectives  14.6 us (31%)
  starting transfers between devices  11.6 us (25%)
  Pallas kernels  10 us (21%)
  waiting for transfers between devices  8.29 us (18%)
  local copies, waits for them, and re-layouts  1.49 us (3%)
    all_to_all x1, blocking collectives, body(): lax.all_to_all(state, ('z', 'yx'), split_axis=0, concat_axis=0, tiled=True)  14.6 us
    all_to_all x1, starting transfers between devices, body(): lax.all_to_all(state, ('z', 'yx', 'core'), split_axis=0, concat_axis=0, t...  11.1 us
    all_to_all x1, waiting for transfers between devices, body(): lax.all_to_all(state, ('z', 'yx', 'core'), split_axis=0, concat_axis=0, t...  7.13 us
    pallas_call x1, Pallas kernels, evolve(): pl.pallas_call(evolve_kernel, out_shape=(jax.ShapeDtypeStruct((32, 2, 16,...  5.05 us
    pallas_call x1, Pallas kernels, prepare(): pl.pallas_call(prepare_kernel, out_shape=(jax.ShapeDtypeStruct((LAYERS, G...  4.97 us
    unnamed x5, local copies, waits for them, and re-layouts  1.46 us
    ppermute x1, waiting for transfers between devices, body(): got = lax.ppermute(sent, 'core', [(0, 1), (1, 0)])  1.16 us
  transfers between devices with their start and end apart: 2, of which 2 were waited for; matrix products, arithmetic and copies ran while one was open for 0% of the time, Pallas kernels for 11%

profile of v7, /device:TPU:1, one launch (start us, length us, event | category | flops | bytes accessed | tf_op | source)
XLA Modules:
  0.0 46.0 jit_solution(3147810062368420476)
XLA Ops:
  0.0 0.0 copy-start
  0.0 11.1 %all-to-all-start = ((f32[64,16,128]{2,1,0:T(8,128)}), f32[64,16,128]{2,1,0:T(8,128)S(1)}, u32[]{:S(2)}, u32[]{:S(2)}) async-start(f32[64,16,128]{2,1,0:T(8,128)} %bitcast.8), calls=%async_computation | async-start | bytes 1048576 | tf_op jit(solution)/shard_map/all_to_all | solution.py:343
  11.1 0.0 copy-start.1
  11.1 0.0 copy-done
  11.1 0.7 %copy-done.1 = s32[8,7]{1,0:T(8,128)S(1)} copy-done((s32[8,7]{1,0:T(8,128)S(1)}, s32[8,7]{1,0:T(8,128)}, u32[]{:S(2)}) %copy-start.1) | copy-done | bytes 248
  11.8 5.0 %prepare.1 = (bf16[8,128,384]{2,1,0:T(8,128)(2,1)S(1)}, s32[16,128]{1,0:T(8,128)S(1)}, bf16[4,128,128]{2,1,0:T(8,128)(2,1)S(1)}) custom-call(s32[8,7]{1,0:T(8,128)S(1)} %copy-done.1, f32[8,128,128]{2,1,0:T(8,128)S(1)} %copy-done), custom_call_target="tpu_custom_call" | custom-call | flops 8000000000 | bytes 20971520 | tf_op jit(solution)/shard_map/prepare/pallas_call | solution.py:206
  16.7 7.1 %all-to-all-done.x_ref = f32[64,16,128]{2,1,0:T(8,128)S(1)} async-done(((f32[64,16,128]{2,1,0:T(8,128)}), f32[64,16,128]{2,1,0:T(8,128)S(1)}, u32[]{:S(2)}, u32[]{:S(2)}) %all-to-all-start) | async-done | bytes 524320 | tf_op jit(solution)/shard_map/all_to_all | solution.py:343
  23.9 5.1 %evolve.1 = (f32[32,2,16,128]{3,2,1,0:T(8,128)S(1)}, f32[32,16,128]{2,1,0:T(8,128)S(1)}) custom-call(s32[1]{0:T(128)} %bitcast.core_ref, f32[64,16,128]{2,1,0:T(8,128)S(1)} %all-to-all-done.x_ref, bf16[8,128,384]{2,1,0:T(8,128)(2,1)S(1)} %get-tuple-element.10.gates_ref, s32[16,128]{1,0:T(8,128)S(1)} %get-tuple-element.11.moves_ref, ...), custom_call_target="tpu_custom_call" | custom-call | flops 6000000000 | bytes 20971520 | tf_op jit(solution)/shard_map/evolve/pallas_call | solution.py:321
  28.9 0.6 %collective-permute-start = (f32[32,16,128]{2,1,0:T(8,128)S(1)}, f32[32,16,128]{2,1,0:T(8,128)S(1)}, u32[]{:S(2)}, u32[]{:S(2)}) collective-permute-start(f32[32,16,128]{2,1,0:T(8,128)S(1)} %get-tuple-element.14), channel_id=1, source_target_pairs={{0,1},{1,0},{2,3},{3,2},{4,5},{5,4},{6,7},{7,6},{8,9},{9,8},{10,11... | collective-permute-start | bytes 786440 | tf_op jit(solution)/shard_map/ppermute | solution.py:345
  29.5 1.2 %collective-permute-done = f32[32,16,128]{2,1,0:T(8,128)S(1)} collective-permute-done((f32[32,16,128]{2,1,0:T(8,128)S(1)}, f32[32,16,128]{2,1,0:T(8,128)S(1)}, u32[]{:S(2)}, u32[]{:S(2)}) %collective-permute-start) | collective-permute-done | bytes 262176 | tf_op jit(solution)/shard_map/ppermute | solution.py:345
  30.7 14.6 %all_to_all.10 = f32[32,2,16,128]{3,2,1,0:T(8,128)S(1)} all-to-all(f32[32,2,16,128]{3,2,1,0:T(8,128)S(1)} %bitcast_dynamic-update-slice_fusion), channel_id=1, replica_groups=mesh['top'=2,'z'=4,'yx'=8,'core'=2] {'z','yx'}, dimensions={0} | all-to-all | bytes 1048576 | tf_op jit(solution)/shard_map/all_to_all | solution.py:347
  45.2 0.8 %copy.7 = f32[1,1,131072]{2,1,0:T(1,128)} copy(f32[1,1,131072]{2,1,0:T(1,128)S(1)} %bitcast.7) | data formatting | bytes 1048576
  (1 shorter events, 0.0 us)
Async XLA Ops:
  0.0 11.1 %copy-start = (f32[8,128,128]{2,1,0:T(8,128)S(1)}, f32[8,128,128]{2,1,0:T(8,128)}, u32[]{:S(2)}) copy-start(f32[8,128,128]{2,1,0:T(8,128)} %stack_ref.1) | copy-start | bytes 1572868
  0.0 23.9 %all-to-all-start = ((f32[64,16,128]{2,1,0:T(8,128)}), f32[64,16,128]{2,1,0:T(8,128)S(1)}, u32[]{:S(2)}, u32[]{:S(2)}) async-start(f32[64,16,128]{2,1,0:T(8,128)} %bitcast.8), calls=%async_computation | async-start | bytes 1048576 | tf_op jit(solution)/shard_map/all_to_all | solution.py:343
  11.1 0.7 %copy-start.1 = (s32[8,7]{1,0:T(8,128)S(1)}, s32[8,7]{1,0:T(8,128)}, u32[]{:S(2)}) copy-start(s32[8,7]{1,0:T(8,128)} %targets_ref.1) | copy-start | bytes 676
  28.9 1.7 %collective-permute-start = (f32[32,16,128]{2,1,0:T(8,128)S(1)}, f32[32,16,128]{2,1,0:T(8,128)S(1)}, u32[]{:S(2)}, u32[]{:S(2)}) collective-permute-start(f32[32,16,128]{2,1,0:T(8,128)S(1)} %get-tuple-element.14), channel_id=1, source_target_pairs={{0,1},{1,0},{2,3},{3,2},{4,5},{5,4},{6,7},{7,6},{8,9},{9,8},{10,11... | collective-permute-start | bytes 786440 | tf_op jit(solution)/shard_map/ppermute | solution.py:345

commit v8 on v7

--- a/solution.py
+++ b/solution.py
@@ -199,14 +199,14 @@
         if g % 4 == 1:
             parts = jnp.where((tall & 64) == 0, parts, pltpu.roll(parts, 64, 1))
         parts = parts.astype(BF16)
-        gates_ref[g] = jnp.concatenate([parts[:GATE], parts[:GATE], parts[GATE:]], 1)
+        gates_ref[g] = jnp.concatenate([parts, parts], 1)
 
 
 def prepare(targets, gate_stack):
     return pl.pallas_call(
         prepare_kernel,
         out_shape=(
-            jax.ShapeDtypeStruct((LAYERS, GATE, 3 * GATE), BF16),
+            jax.ShapeDtypeStruct((LAYERS, 2 * GATE, 2 * GATE), BF16),
             jax.ShapeDtypeStruct((16, GATE), I32),
             jax.ShapeDtypeStruct((4, GATE, GATE), BF16),
         ),
@@ -262,8 +262,8 @@
         return jnp.concatenate([source[pl.ds(pl.multiple_of(place, 8), 8), :] for place in places], 0)
 
     def applied(layer, blocks):
-        stacked = side_by_side(blocks)
-        return dot(gates_ref[layer], jnp.concatenate([stacked, stacked[:GATE]], 0))
+        out = dot(gates_ref[layer], side_by_side(blocks))
+        return out[:GATE] + out[GATE:]
 
     source, target = here, there
     for layer in range(LAYERS):

time: 46.7 us -> 46.7 us (level)
  no operation moved by 1% of the time
where the time goes in v8:
time: 46.7 us; the launch traced here: 46.1 us
  blocking collectives  14.6 us (31%)
  starting transfers between devices  11.6 us (25%)
  Pallas kernels  10.1 us (22%)
  waiting for transfers between devices  8.29 us (18%)
  local copies, waits for them, and re-layouts  1.49 us (3%)
    all_to_all x1, blocking collectives, body(): lax.all_to_all(state, ('z', 'yx'), split_axis=0, concat_axis=0, tiled=True)  14.6 us
    all_to_all x1, starting transfers between devices, body(): lax.all_to_all(state, ('z', 'yx', 'core'), split_axis=0, concat_axis=0, t...  11.1 us
    all_to_all x1, waiting for transfers between devices, body(): lax.all_to_all(state, ('z', 'yx', 'core'), split_axis=0, concat_axis=0, t...  7.13 us
    pallas_call x1, Pallas kernels, evolve(): pl.pallas_call(evolve_kernel, out_shape=(jax.ShapeDtypeStruct((32, 2, 16,...  5.09 us
    pallas_call x1, Pallas kernels, prepare(): pl.pallas_call(prepare_kernel, out_shape=(jax.ShapeDtypeStruct((LAYERS, 2...  4.97 us
    unnamed x5, local copies, waits for them, and re-layouts  1.46 us
    ppermute x1, waiting for transfers between devices, body(): got = lax.ppermute(sent, 'core', [(0, 1), (1, 0)])  1.16 us
  transfers between devices with their start and end apart: 2, of which 2 were waited for; matrix products, arithmetic and copies ran while one was open for 0% of the time, Pallas kernels for 11%

profile of v8, /device:TPU:1, one launch (start us, length us, event | category | flops | bytes accessed | tf_op | source)
XLA Modules:
  0.0 46.1 jit_solution(8927616963673345576)
XLA Ops:
  0.0 0.0 copy-start
  0.0 11.1 %all-to-all-start = ((f32[64,16,128]{2,1,0:T(8,128)}), f32[64,16,128]{2,1,0:T(8,128)S(1)}, u32[]{:S(2)}, u32[]{:S(2)}) async-start(f32[64,16,128]{2,1,0:T(8,128)} %bitcast.8), calls=%async_computation | async-start | bytes 1048576 | tf_op jit(solution)/shard_map/all_to_all | solution.py:343
  11.1 0.0 copy-start.1
  11.1 0.0 copy-done
  11.1 0.7 %copy-done.1 = s32[8,7]{1,0:T(8,128)S(1)} copy-done((s32[8,7]{1,0:T(8,128)S(1)}, s32[8,7]{1,0:T(8,128)}, u32[]{:S(2)}) %copy-start.1) | copy-done | bytes 248
  11.8 5.0 %prepare.1 = (bf16[8,256,256]{2,1,0:T(8,128)(2,1)S(1)}, s32[16,128]{1,0:T(8,128)S(1)}, bf16[4,128,128]{2,1,0:T(8,128)(2,1)S(1)}) custom-call(s32[8,7]{1,0:T(8,128)S(1)} %copy-done.1, f32[8,128,128]{2,1,0:T(8,128)S(1)} %copy-done), custom_call_target="tpu_custom_call" | custom-call | flops 8000000000 | bytes 20971520 | tf_op jit(solution)/shard_map/prepare/pallas_call | solution.py:206
  16.7 7.1 %all-to-all-done.x_ref = f32[64,16,128]{2,1,0:T(8,128)S(1)} async-done(((f32[64,16,128]{2,1,0:T(8,128)}), f32[64,16,128]{2,1,0:T(8,128)S(1)}, u32[]{:S(2)}, u32[]{:S(2)}) %all-to-all-start) | async-done | bytes 524320 | tf_op jit(solution)/shard_map/all_to_all | solution.py:343
  23.9 5.1 %evolve.1 = (f32[32,2,16,128]{3,2,1,0:T(8,128)S(1)}, f32[32,16,128]{2,1,0:T(8,128)S(1)}) custom-call(s32[1]{0:T(128)} %bitcast.core_ref, f32[64,16,128]{2,1,0:T(8,128)S(1)} %all-to-all-done.x_ref, bf16[8,256,256]{2,1,0:T(8,128)(2,1)S(1)} %get-tuple-element.10.gates_ref, s32[16,128]{1,0:T(8,128)S(1)} %get-tuple-element.11.moves_ref, ...), custom_call_target="tpu_custom_call" | custom-call | flops 6000000000 | bytes 20971520 | tf_op jit(solution)/shard_map/evolve/pallas_call | solution.py:321
  29.0 0.6 %collective-permute-start = (f32[32,16,128]{2,1,0:T(8,128)S(1)}, f32[32,16,128]{2,1,0:T(8,128)S(1)}, u32[]{:S(2)}, u32[]{:S(2)}) collective-permute-start(f32[32,16,128]{2,1,0:T(8,128)S(1)} %get-tuple-element.14), channel_id=1, source_target_pairs={{0,1},{1,0},{2,3},{3,2},{4,5},{5,4},{6,7},{7,6},{8,9},{9,8},{10,11... | collective-permute-start | bytes 786440 | tf_op jit(solution)/shard_map/ppermute | solution.py:345
  29.5 1.2 %collective-permute-done = f32[32,16,128]{2,1,0:T(8,128)S(1)} collective-permute-done((f32[32,16,128]{2,1,0:T(8,128)S(1)}, f32[32,16,128]{2,1,0:T(8,128)S(1)}, u32[]{:S(2)}, u32[]{:S(2)}) %collective-permute-start) | collective-permute-done | bytes 262176 | tf_op jit(solution)/shard_map/ppermute | solution.py:345
  30.7 14.6 %all_to_all.10 = f32[32,2,16,128]{3,2,1,0:T(8,128)S(1)} all-to-all(f32[32,2,16,128]{3,2,1,0:T(8,128)S(1)} %bitcast_dynamic-update-slice_fusion), channel_id=1, replica_groups=mesh['top'=2,'z'=4,'yx'=8,'core'=2] {'z','yx'}, dimensions={0} | all-to-all | bytes 1048576 | tf_op jit(solution)/shard_map/all_to_all | solution.py:347
  45.3 0.8 %copy.7 = f32[1,1,131072]{2,1,0:T(1,128)} copy(f32[1,1,131072]{2,1,0:T(1,128)S(1)} %bitcast.7) | data formatting | bytes 1048576
  (1 shorter events, 0.0 us)
Async XLA Ops:
  0.0 11.1 %copy-start = (f32[8,128,128]{2,1,0:T(8,128)S(1)}, f32[8,128,128]{2,1,0:T(8,128)}, u32[]{:S(2)}) copy-start(f32[8,128,128]{2,1,0:T(8,128)} %stack_ref.1) | copy-start | bytes 1572868
  0.0 23.9 %all-to-all-start = ((f32[64,16,128]{2,1,0:T(8,128)}), f32[64,16,128]{2,1,0:T(8,128)S(1)}, u32[]{:S(2)}, u32[]{:S(2)}) async-start(f32[64,16,128]{2,1,0:T(8,128)} %bitcast.8), calls=%async_computation | async-start | bytes 1048576 | tf_op jit(solution)/shard_map/all_to_all | solution.py:343
  11.1 0.7 %copy-start.1 = (s32[8,7]{1,0:T(8,128)S(1)}, s32[8,7]{1,0:T(8,128)}, u32[]{:S(2)}) copy-start(s32[8,7]{1,0:T(8,128)} %targets_ref.1) | copy-start | bytes 676
  29.0 1.7 %collective-permute-start = (f32[32,16,128]{2,1,0:T(8,128)S(1)}, f32[32,16,128]{2,1,0:T(8,128)S(1)}, u32[]{:S(2)}, u32[]{:S(2)}) collective-permute-start(f32[32,16,128]{2,1,0:T(8,128)S(1)} %get-tuple-element.14), channel_id=1, source_target_pairs={{0,1},{1,0},{2,3},{3,2},{4,5},{5,4},{6,7},{7,6},{8,9},{9,8},{10,11... | collective-permute-start | bytes 786440 | tf_op jit(solution)/shard_map/ppermute | solution.py:345
